TPU v7x, 128 devices: a whole 4x4x4 slice. The times are simulated.
128 devices in a mesh: ctx: 8 (over y, x_hi), head: 16 (over x_lo, z, core).
Axes of the slice: x: 4 (x_hi: 2, x_lo: 2; x = x_hi * 2 + x_lo), y: 4, z: 4, core: 2. Of those that a mesh axis runs over, the one named last changes fastest.
Arguments:
- query: bfloat16 [16384, 32, 128], P(('ctx', 'head')), may hold values from -6 to 6
- keys: bfloat16 [16384, 32, 128], P(('ctx', 'head')), may hold values from -6 to 6
- values: bfloat16 [16384, 32, 128], P(('ctx', 'head')), may hold values from -6 to 6
- grad_out: bfloat16 [16384, 32, 128], P(('ctx', 'head')), may hold values from -6 to 6
- window: int32 [32], P('head'), may hold values from 1 to 8, as said below
- global_blocks: int32 [6], replicated, may hold values from 0 to 127, as said below
Outputs:
- attended: bfloat16 [16384, 32, 128], P(('ctx', 'head'))
- grad_query: bfloat16 [16384, 32, 128], P(('ctx', 'head'))
- grad_keys: bfloat16 [16384, 32, 128], P(('ctx', 'head'))
- grad_values: bfloat16 [16384, 32, 128], P(('ctx', 'head'))
Inputs may be any that keep to these rules, and one draw needn't show every extreme that they name: Some head has a window of exactly 8 blocks. `global_blocks`: 6 distinct block indices; blocks 0 and 127 are always among them.
All inputs are finite; a program needn't handle non-finite values.
Results may differ from a plain program's by a relative error of at most 0.019.
Values may be sent and summed in bfloat16 or wider, within the bound.
No kernel may reach another device: no remote copies, remote signals or barrier semaphores. Data moves between devices by JAX's collectives and lax.ppermute only.
A program may use at most 128 MiB of HBM per device.

v0:
```python
import jax
import jax.numpy as jnp
from jax import lax
from jax.sharding import PartitionSpec as P

BLK = 128


NEG_FILL = -1e30


def padded(block, sides, width):
    for axis, dim in sides:
        count = lax.axis_size(axis)
        forward = [(i, i + 1) for i in range(count - 1)]
        backward = [(target, source) for source, target in forward]
        low = lax.ppermute(
            lax.slice_in_dim(block, block.shape[dim] - width, None, axis=dim), axis, forward
        )
        high = lax.ppermute(lax.slice_in_dim(block, 0, width, axis=dim), axis, backward)
        block = jnp.concatenate([low, block, high], axis=dim)
    return block


def rows_by_cols(left, right):
    return lax.dot_general(
        left, right, (((1,), (1,)), ((), ())), preferred_element_type=jnp.float32
    )


def cols_by_rows(left, right):
    return lax.dot_general(
        left, right, (((0,), (0,)), ((), ())), preferred_element_type=jnp.float32
    )


def head_masks(first, segment, width, glob_cols):
    query_pos = first + jnp.arange(segment, dtype=jnp.int32)
    key_pos = first - segment + jnp.arange(2 * segment, dtype=jnp.int32)
    query_blk = query_pos // BLK
    band_ok = (
        (key_pos[None, :] >= 0)
        & (key_pos[None, :] <= query_pos[:, None])
        & (query_blk[:, None] - key_pos[None, :] // BLK < width)
    )
    glob_ok = glob_cols[None, :] <= query_blk[:, None] - width
    return (band_ok, glob_ok)


def scores_of(query_rows, band_keys, glob_keys, band_ok, glob_ok, scale):
    band_s = jnp.where(band_ok, rows_by_cols(query_rows, band_keys) * scale, NEG_FILL)
    glob_s = jnp.where(glob_ok, rows_by_cols(query_rows, glob_keys) * scale, NEG_FILL)
    return (band_s, glob_s)


def forward_rows(query_rows, band_keys, band_vals, glob_keys, glob_vals, band_ok, glob_ok, scale):
    band_s, glob_s = scores_of(query_rows, band_keys, glob_keys, band_ok, glob_ok, scale)
    top = jnp.maximum(jnp.max(band_s, axis=1), jnp.max(glob_s, axis=1))
    total = jnp.sum(jnp.exp(band_s - top[:, None]), axis=1) + jnp.sum(
        jnp.exp(glob_s - top[:, None]), axis=1
    )
    log_total = top + jnp.log(total)
    band_w = jnp.exp(band_s - log_total[:, None]).astype(jnp.bfloat16)
    glob_w = jnp.exp(glob_s - log_total[:, None]).astype(jnp.bfloat16)
    result = jnp.dot(band_w, band_vals, preferred_element_type=jnp.float32) + jnp.dot(
        glob_w, glob_vals, preferred_element_type=jnp.float32
    )
    return (result.astype(jnp.bfloat16), log_total)


def backward_rows(
    query_rows,
    band_keys,
    band_vals,
    glob_keys,
    glob_vals,
    band_ok,
    glob_ok,
    scale,
    log_total,
    attended_rows,
    grad_rows,
):
    band_s, glob_s = scores_of(query_rows, band_keys, glob_keys, band_ok, glob_ok, scale)
    band_p = jnp.exp(band_s - log_total[:, None])
    glob_p = jnp.exp(glob_s - log_total[:, None])
    delta = jnp.sum(grad_rows.astype(jnp.float32) * attended_rows.astype(jnp.float32), axis=1)
    band_ds = (band_p * (rows_by_cols(grad_rows, band_vals) - delta[:, None])).astype(jnp.bfloat16)
    glob_ds = (glob_p * (rows_by_cols(grad_rows, glob_vals) - delta[:, None])).astype(jnp.bfloat16)
    band_w = band_p.astype(jnp.bfloat16)
    glob_w = glob_p.astype(jnp.bfloat16)
    grad_query = (
        jnp.dot(band_ds, band_keys, preferred_element_type=jnp.float32)
        + jnp.dot(glob_ds, glob_keys, preferred_element_type=jnp.float32)
    ) * scale
    band_dk = cols_by_rows(band_ds, query_rows) * scale
    band_dv = cols_by_rows(band_w, grad_rows)
    glob_dk = cols_by_rows(glob_ds, query_rows) * scale
    glob_dv = cols_by_rows(glob_w, grad_rows)
    return (grad_query.astype(jnp.bfloat16), band_dk, band_dv, glob_dk, glob_dv)


def shards(query, keys, values, grad_out, window, global_blocks):
    q_local, k_local, v_local, d_local = (
        lax.all_to_all(query, "head", split_axis=1, concat_axis=0, tiled=True),
        lax.all_to_all(keys, "head", split_axis=1, concat_axis=0, tiled=True),
        lax.all_to_all(values, "head", split_axis=1, concat_axis=0, tiled=True),
        lax.all_to_all(grad_out, "head", split_axis=1, concat_axis=0, tiled=True),
    )
    tokens = q_local.shape[0]
    segment = tokens // 2
    heads = q_local.shape[1]
    scale = q_local.shape[2] ** (-0.5)
    ctx_pos = lax.axis_index("ctx")
    ctx_count = lax.axis_size("ctx")
    pair = jnp.stack([k_local, v_local])
    swapped = jnp.concatenate([pair[:, segment:], pair[:, :segment]], axis=1)
    extended = padded(swapped, (("ctx", 1),), segment)
    before_first = extended[:, :segment]
    before_second = jnp.where(
        ctx_pos == ctx_count - 1, pair[:, :segment], extended[:, segment + tokens :]
    )
    start_row = global_blocks * BLK
    segment_id = start_row // segment
    in_first = segment_id < ctx_count
    owner = jnp.where(in_first, segment_id, 2 * ctx_count - 1 - segment_id)
    offset = jnp.where(in_first, 0, segment) + start_row - segment_id * segment
    row_index = (offset[:, None] + jnp.arange(BLK, dtype=jnp.int32)[None, :]).reshape(-1)
    row_mine = jnp.repeat(owner == ctx_pos, BLK)
    glob_cols = jnp.repeat(global_blocks, BLK)
    picked = jnp.where(row_mine[:, None, None][None], pair[:, row_index], 0).astype(jnp.float32)
    glob_pair = lax.psum(picked.astype(jnp.bfloat16), "ctx")
    firsts = (ctx_pos * segment, (2 * ctx_count - 1 - ctx_pos) * segment)
    bands = (
        jnp.concatenate([before_first, pair[:, :segment]], axis=1),
        jnp.concatenate([before_second, pair[:, segment:]], axis=1),
    )
    masks = []
    log_parts = []
    attended_parts = []
    for portion in range(2):
        rows_here = q_local[portion * segment : (portion + 1) * segment]
        head_rows = []
        for head_slot in range(heads):
            band_ok, glob_ok = head_masks(firsts[portion], segment, window[head_slot], glob_cols)
            masks.append((band_ok, glob_ok))
            result, log_total = forward_rows(
                rows_here[:, head_slot],
                bands[portion][0, :, head_slot],
                bands[portion][1, :, head_slot],
                glob_pair[0, :, head_slot],
                glob_pair[1, :, head_slot],
                band_ok,
                glob_ok,
                scale,
            )
            head_rows.append(result)
            log_parts.append(log_total)
        attended_parts.append(jnp.stack(head_rows, axis=1))
    attended = jnp.concatenate(attended_parts, axis=0)
    query_parts = []
    band_grads = []
    glob_terms = []
    for portion in range(2):
        rows_here = q_local[portion * segment : (portion + 1) * segment]
        grads_here = d_local[portion * segment : (portion + 1) * segment]
        head_dq, head_dk, head_dv = ([], [], [])
        for head_slot in range(heads):
            band_ok, glob_ok = masks[portion * heads + head_slot]
            grad_query, band_dk, band_dv, glob_dk, glob_dv = backward_rows(
                rows_here[:, head_slot],
                bands[portion][0, :, head_slot],
                bands[portion][1, :, head_slot],
                glob_pair[0, :, head_slot],
                glob_pair[1, :, head_slot],
                band_ok,
                glob_ok,
                scale,
                log_parts[portion * heads + head_slot],
                attended_parts[portion][:, head_slot],
                grads_here[:, head_slot],
            )
            head_dq.append(grad_query)
            head_dk.append(band_dk)
            head_dv.append(band_dv)
            glob_terms.append((head_slot, glob_dk, glob_dv))
        query_parts.append(jnp.stack(head_dq, axis=1))
        band_grads.append(jnp.stack([jnp.stack(head_dk, axis=1), jnp.stack(head_dv, axis=1)]))
    glob_keys_grad = []
    glob_vals_grad = []
    for head_slot in range(heads):
        glob_keys_grad.append(glob_terms[head_slot][1] + glob_terms[heads + head_slot][1])
        glob_vals_grad.append(glob_terms[head_slot][2] + glob_terms[heads + head_slot][2])
    glob_grad = jnp.stack([jnp.stack(glob_keys_grad, axis=1), jnp.stack(glob_vals_grad, axis=1)])
    to_prev = jnp.concatenate([band_grads[0][:, :segment], band_grads[1][:, :segment]], axis=1)
    returned = padded(to_prev.astype(jnp.bfloat16), (("ctx", 1),), segment).astype(to_prev.dtype)
    from_left = returned[:, :segment]
    from_right = returned[:, segment + tokens :]
    grad_first = (
        band_grads[0][:, segment:]
        + from_right
        + jnp.where(ctx_pos == ctx_count - 1, band_grads[1][:, :segment], 0.0)
    )
    grad_second = band_grads[1][:, segment:] + from_left
    glob_total = lax.psum(glob_grad.astype(jnp.bfloat16), "ctx").astype(jnp.float32)
    grad_pair = jnp.concatenate([grad_first, grad_second], axis=1)
    grad_pair = grad_pair.at[:, row_index].add(
        jnp.where(row_mine[:, None, None][None], glob_total, 0.0)
    )
    grad_pair = grad_pair.astype(jnp.bfloat16)
    grad_query_all = jnp.concatenate(query_parts, axis=0)
    attended_out, query_out, keys_out, values_out = (
        lax.all_to_all(attended, "head", split_axis=0, concat_axis=1, tiled=True),
        lax.all_to_all(grad_query_all, "head", split_axis=0, concat_axis=1, tiled=True),
        lax.all_to_all(grad_pair[0], "head", split_axis=0, concat_axis=1, tiled=True),
        lax.all_to_all(grad_pair[1], "head", split_axis=0, concat_axis=1, tiled=True),
    )
    return (attended_out, query_out, keys_out, values_out)


def solution(mesh):
    return jax.shard_map(
        shards,
        mesh=mesh,
        in_specs=(
            P(("ctx", "head"), None, None),
            P(("ctx", "head"), None, None),
            P(("ctx", "head"), None, None),
            P(("ctx", "head"), None, None),
            P("head"),
            P(),
        ),
        out_specs=(
            P(("ctx", "head"), None, None),
            P(("ctx", "head"), None, None),
            P(("ctx", "head"), None, None),
            P(("ctx", "head"), None, None),
        ),
        check_vma=False,
    )
```

profile of v0, /device:TPU:1, one launch (start us, length us, event | category | flops | bytes accessed | tf_op | source)
XLA Modules:
  0.0 587.6 jit_solution(11766188314092811497)
XLA Ops:
  7.2 2.7 copy.40
  9.9 7.9 %all-to-all-start = ((bf16[128,32,128]{2,0,1:T(8,128)(2,1)}), bf16[128,32,128]{2,0,1:T(8,128)(2,1)S(1)}, u32[]{:S(2)}, u32[]{:S(2)}) async-start(bf16[128,32,128]{2,0,1:T(8,128)(2,1)} %copy.40), calls=%async_computation | async-start | bytes 2097152 | tf_op jit(solution)/shard_map/all_to_all | solution.py:106
  19.1 14.4 %all-to-all-done = bf16[128,32,128]{2,0,1:T(8,128)(2,1)S(1)} async-done(((bf16[128,32,128]{2,0,1:T(8,128)(2,1)}), bf16[128,32,128]{2,0,1:T(8,128)(2,1)S(1)}, u32[]{:S(2)}, u32[]{:S(2)}) %all-to-all-start) | async-done | bytes 1048608 | tf_op jit(solution)/shard_map/all_to_all | solution.py:106
  33.6 4.3 all-to-all-start.1
  39.3 2.6 copy.50
  42.7 11.1 %all-to-all-done.1 = bf16[128,32,128]{2,0,1:T(8,128)(2,1)S(1)} async-done(((bf16[128,32,128]{2,0,1:T(8,128)(2,1)}), bf16[128,32,128]{2,0,1:T(8,128)(2,1)S(1)}, u32[]{:S(2)}, u32[]{:S(2)}) %all-to-all-start.1) | async-done | bytes 1048608 | tf_op jit(solution)/shard_map/all_to_all | solution.py:107
  53.8 4.9 all-to-all-start.2
  63.1 11.6 %all-to-all-done.2 = bf16[128,32,128]{2,0,1:T(8,128)(2,1)} async-done(((bf16[128,32,128]{2,0,1:T(8,128)(2,1)}), bf16[128,32,128]{2,0,1:T(8,128)(2,1)}, u32[]{:S(2)}, u32[]{:S(2)}) %all-to-all-start.2) | async-done | bytes 1048608 | tf_op jit(solution)/shard_map/all_to_all | solution.py:105
  74.8 4.9 all-to-all-start.4
  80.0 18.1 %copy.46 = bf16[2,2048,2,128]{3,2,1,0:T(2,128)(2,1)} copy(bf16[2,2048,2,128]{3,1,2,0:T(8,128)(2,1)S(1)} %pad_maximum_fusion.1) | data formatting | bytes 4194304 | tf_op jit(solution)/shard_map/stack | solution.py:116
  98.1 4.5 gather_fusion
  102.6 3.5 fusion.66
  113.4 80.7 %all-reduce.3.cloned.1.call-done = bf16[2,768,2,128]{3,2,0,1:T(2,128)(2,1)} async-done(((bf16[2,768,2,128]{3,2,0,1:T(2,128)(2,1)}), bf16[2,768,2,128]{3,2,0,1:T(2,128)(2,1)}) %all-reduce.3.cloned.1.call-update) | async-done | bytes 786448 | tf_op jit(solution)/shard_map/psum | solution.py:132
  194.2 2.7 fusion.151
  203.5 4.0 fusion.153
  207.5 3.9 fusion.155
  213.5 2.3 fusion.82
  215.9 2.4 convolution_bitcast_fusion
  219.9 2.9 fusion.41
  224.1 2.4 multiply_reduce_fusion.1
  226.5 4.8 fusion
  233.2 2.4 convolution_bitcast_fusion.1
  235.6 2.1 fusion.13
  237.7 3.0 fusion.1
  240.7 2.2 collective-permute-start
  250.7 5.5 collective-permute-start.2
  260.9 3.9 fusion.159
  269.3 2.4 convolution_bitcast_fusion.3
  271.7 4.4 fusion.157
  277.7 2.4 fusion.87
  289.1 2.4 convolution_bitcast_fusion.2
  294.3 3.0 fusion.3
  308.4 9.5 %copy.48 = bf16[2048,2,128]{2,1,0:T(2,128)(2,1)} copy(bf16[2048,2,128]{2,0,1:T(8,128)(2,1)S(1)} %maximum_maximum_fusion) | data formatting | bytes 2097152 | tf_op jit(solution)/shard_map/concatenate | solution.py:160
  318.9 15.8 %all-to-all-start.3 = ((bf16[2048,2,128]{2,1,0:T(2,128)(2,1)}), bf16[2048,2,128]{2,1,0:T(2,128)(2,1)}, u32[]{:S(2)}, u32[]{:S(2)}) async-start(bf16[2048,2,128]{2,1,0:T(2,128)(2,1)} %copy.48), calls=%async_computation.3 | async-start | bytes 2097152 | tf_op jit(solution)/shard_map/all_to_all | solution.py:213
  334.8 3.6 fusion.48
  340.6 9.5 %copy.52 = bf16[2048,2,128]{2,1,0:T(2,128)(2,1)} copy(bf16[2048,2,128]{2,0,1:T(8,128)(2,1)S(1)} %maximum_maximum_fusion.1) | data formatting | bytes 2097152 | tf_op jit(solution)/shard_map/concatenate | solution.py:211
  350.0 71.8 %all-reduce.5.cloned.1.call-done = bf16[2,768,2,128]{3,1,2,0:T(8,128)(2,1)} async-done(((bf16[2,768,2,128]{3,1,2,0:T(8,128)(2,1)}), bf16[2,768,2,128]{3,1,2,0:T(8,128)(2,1)}) %all-reduce.5.cloned.1.call-update) | async-done | bytes 786448 | tf_op jit(solution)/shard_map/psum | solution.py:205
  423.2 2.4 copy.55
  425.6 10.5 %all-to-all-start.5 = ((bf16[2048,2,128]{2,1,0:T(2,128)(2,1)}), bf16[2048,2,128]{2,1,0:T(2,128)(2,1)S(1)}, u32[]{:S(2)}, u32[]{:S(2)}) async-start(bf16[2048,2,128]{2,1,0:T(2,128)(2,1)} %copy.52), calls=%async_computation.5 | async-start | bytes 2097152 | tf_op jit(solution)/shard_map/all_to_all | solution.py:214
  436.1 3.0 fusion.27
  439.4 16.1 %copy.54 = f32[2,2048,2,128]{3,2,1,0:T(2,128)} copy(f32[2,2048,2,128]{3,1,2,0:T(8,128)S(1)} %pad_maximum_fusion) | data formatting | bytes 8388608 | tf_op jit(solution)/shard_map/concatenate | solution.py:206
  455.6 75.7 %scatter_fusion = f32[2,2048,2,128]{3,2,1,0:T(2,128)} fusion(f32[2,2048,2,128]{3,2,1,0:T(2,128)} %copy.54, s32[768]{0:T(1024)S(1)} %copy-done.64, f32[768,2,2,128]{3,2,1,0:T(2,128)S(1)} %copy-done.24), kind=kCustom, calls=%fused_computation.1 | custom fusion | flops 393216 | bytes 4721664 | tf_op jit(solution)/shard_map/scatter-add | solution.py:207
  531.3 3.6 convert_element_type.153
  534.9 2.3 slice_bitcast_fusion
  537.2 20.9 %all_to_all.132 = bf16[2048,2,128]{2,1,0:T(2,128)(2,1)S(1)} all-to-all(bf16[2048,2,128]{2,1,0:T(2,128)(2,1)S(1)} %get-tuple-element.14), channel_id=1, replica_groups=mesh['ctx'=8,'head'=16] {'head'}, dimensions={0} | all-to-all | bytes 2097152 | tf_op jit(solution)/shard_map/all_to_all | solution.py:216
  558.2 4.6 all-to-all-start.6
  562.8 2.9 copy.49
  569.1 9.6 %all-to-all-done.6 = bf16[2048,2,128]{2,1,0:T(2,128)(2,1)S(1)} async-done(((bf16[2048,2,128]{2,1,0:T(2,128)(2,1)}), bf16[2048,2,128]{2,1,0:T(2,128)(2,1)S(1)}, u32[]{:S(2)}, u32[]{:S(2)}) %all-to-all-start.6) | async-done | bytes 1048608 | tf_op jit(solution)/shard_map/all_to_all | solution.py:215
  (248 shorter events, 79.6 us)
Async XLA Ops:
  7.2 10.6 %copy-start.61 = (bf16[128,32,128]{2,1,0:T(8,128)(2,1)S(1)}, bf16[128,32,128]{2,1,0:T(8,128)(2,1)}, u32[]{:S(2)}) copy-start(bf16[128,32,128]{2,1,0:T(8,128)(2,1)} %param.8) | copy-start | bytes 3145732
  9.9 28.0 %copy-start.68 = (s32[6]{0:T(128)S(1)}, s32[6]{0:T(128)}, u32[]{:S(2)}) copy-start(s32[6]{0:T(128)} %param.11) | copy-start | bytes 76
  9.9 28.1 %copy-start.62 = (bf16[128,32,128]{2,1,0:T(8,128)(2,1)S(1)}, bf16[128,32,128]{2,1,0:T(8,128)(2,1)}, u32[]{:S(2)}) copy-start(bf16[128,32,128]{2,1,0:T(8,128)(2,1)} %param.6) | copy-start | bytes 3145732
  9.9 23.7 %all-to-all-start = ((bf16[128,32,128]{2,0,1:T(8,128)(2,1)}), bf16[128,32,128]{2,0,1:T(8,128)(2,1)S(1)}, u32[]{:S(2)}, u32[]{:S(2)}) async-start(bf16[128,32,128]{2,0,1:T(8,128)(2,1)} %copy.40), calls=%async_computation | async-start | bytes 2097152 | tf_op jit(solution)/shard_map/all_to_all | solution.py:106
  19.1 22.9 %copy-start.67 = (s32[2]{0:T(128)S(1)}, s32[2]{0:T(128)}, u32[]{:S(2)}) copy-start(s32[2]{0:T(128)} %param.10) | copy-start | bytes 28
  33.6 20.2 %all-to-all-start.1 = ((bf16[128,32,128]{2,0,1:T(8,128)(2,1)}), bf16[128,32,128]{2,0,1:T(8,128)(2,1)S(1)}, u32[]{:S(2)}, u32[]{:S(2)}) async-start(bf16[128,32,128]{2,0,1:T(8,128)(2,1)} %copy.42), calls=%async_computation.1 | async-start | bytes 2097152 | tf_op jit(solution)/shard_map/all_to_all | solution.py:107
  53.8 7.6 %copy-start.43 = (bf16[128,32,128]{2,0,1:T(8,128)(2,1)}, bf16[128,32,128]{2,0,1:T(8,128)(2,1)S(1)}, u32[]{:S(2)}) copy-start(bf16[128,32,128]{2,0,1:T(8,128)(2,1)S(1)} %all-to-all-done.1) | copy-start | bytes 3145732
  53.8 21.0 %all-to-all-start.2 = ((bf16[128,32,128]{2,0,1:T(8,128)(2,1)}), bf16[128,32,128]{2,0,1:T(8,128)(2,1)}, u32[]{:S(2)}, u32[]{:S(2)}) async-start(bf16[128,32,128]{2,0,1:T(8,128)(2,1)} %copy.44), calls=%async_computation.2 | async-start | bytes 2097152 | tf_op jit(solution)/shard_map/all_to_all | solution.py:105
  61.3 41.3 %copy-start.65 = (pred[768]{0:T(1024)(128)(4,1)}, pred[768]{0:T(1024)(128)(4,1)S(1)}, u32[]{:S(2)}) copy-start(pred[768]{0:T(1024)(128)(4,1)S(1)} %broadcast_bitcast_fusion.1) | copy-start | bytes 2308
  61.4 48.4 %copy-start.15 = (bf16[128,16,2,128]{3,0,1,2:T(8,128)(2,1)}, bf16[128,16,2,128]{3,0,1,2:T(8,128)(2,1)S(1)}, u32[]{:S(2)}) copy-start(bf16[128,16,2,128]{3,0,1,2:T(8,128)(2,1)S(1)} %copy.41) | copy-start | bytes 3145732
  63.1 16.8 %copy-start.17 = (bf16[128,16,2,128]{3,0,1,2:T(8,128)(2,1)}, bf16[128,16,2,128]{3,0,1,2:T(8,128)(2,1)S(1)}, u32[]{:S(2)}) copy-start(bf16[128,16,2,128]{3,0,1,2:T(8,128)(2,1)S(1)} %copy.43) | copy-start | bytes 3145732
  74.8 33.6 %all-to-all-start.4 = ((bf16[128,32,128]{2,0,1:T(8,128)(2,1)}), bf16[128,32,128]{2,0,1:T(8,128)(2,1)}, u32[]{:S(2)}, u32[]{:S(2)}) async-start(bf16[128,32,128]{2,0,1:T(8,128)(2,1)} %copy.50), calls=%async_computation.4 | async-start | bytes 2097152 | tf_op jit(solution)/shard_map/all_to_all | solution.py:108
  79.7 114.5 %all-reduce.3.cloned.1.call-start = ((), (), s32[]{:S(2)}) async-start(), calls=%async_computation.8 | async-start | bytes 1572864 | tf_op jit(solution)/shard_map/psum | solution.py:132
  106.1 315.7 %all-reduce.5.cloned.1.call-start = ((), (), s32[]{:S(2)}) async-start(), calls=%async_computation.9 | async-start | bytes 1572864 | tf_op jit(solution)/shard_map/psum | solution.py:205
  108.4 91.3 %copy-start.34 = (bf16[8,128,2,128]{3,1,0,2:T(8,128)(2,1)}, bf16[8,128,2,128]{3,1,0,2:T(8,128)(2,1)S(1)}, u32[]{:S(2)}) copy-start(bf16[8,128,2,128]{3,1,0,2:T(8,128)(2,1)S(1)} %copy.47) | copy-start | bytes 1572868
  111.0 89.9 %collective-permute-start.1 = (bf16[2,1024,2,128]{3,1,2,0:T(8,128)(2,1)S(1)}, bf16[2,1024,2,128]{3,1,2,0:T(8,128)(2,1)}, u32[]{:S(2)}, u32[]{:S(2)}) collective-permute-start(bf16[2,1024,2,128]{3,1,2,0:T(8,128)(2,1)S(1)} %fusion.65), channel_id=1, source_target_pairs={{16,0},{32,16},{48,32},{64,48},{80,64},{96,80},{112,96},{17,1},{33... | collective-permute-start | bytes 3145736 | tf_op jit(solution)/shard_map/ppermute | solution.py:20
  196.9 2.7 copy-start.53
  202.6 4.9 copy-start.4
  219.9 3.0 copy-start.27
  222.8 3.7 copy-start.30
  226.5 4.8 copy-start.25
  237.7 7.2 %copy-start.3 = (bf16[1024,2048]{0,1:T(8,128)(2,1)S(1)}, bf16[1024,2048]{0,1:T(8,128)(2,1)}, u32[]{:S(2)}) copy-start(bf16[1024,2048]{0,1:T(8,128)(2,1)} %fusion) | copy-start | bytes 12582916
  237.7 7.2 %copy-start.36 = (bf16[8,128,2,128]{3,1,0,2:T(8,128)(2,1)S(1)}, bf16[8,128,2,128]{3,1,0,2:T(8,128)(2,1)}, u32[]{:S(2)}) copy-start(bf16[8,128,2,128]{3,1,0,2:T(8,128)(2,1)} %copy-done.34) | copy-start | bytes 1572868
  240.7 20.2 %collective-permute-start = (bf16[2,1024,2,128]{3,1,2,0:T(8,128)(2,1)S(1)}, bf16[2,1024,2,128]{3,1,2,0:T(8,128)(2,1)S(1)}, u32[]{:S(2)}, u32[]{:S(2)}) collective-permute-start(bf16[2,1024,2,128]{3,1,2,0:T(8,128)(2,1)S(1)} %get-tuple-element.9), channel_id=1, source_target_pairs={{0,16},{16,32},{32,48},{48,64},{64,80},{80,96},{96,112},{1,17},{17... | collective-permute-start | bytes 3145736 | tf_op jit(solution)/shard_map/ppermute | solution.py:17
  249.2 11.7 %copy-start.10 = (f32[1,2048,2,128]{3,1,2,0:T(8,128)}, f32[1,2048,2,128]{3,1,2,0:T(8,128)S(1)}, u32[]{:S(2)}) copy-start(f32[1,2048,2,128]{3,1,2,0:T(8,128)S(1)} %maximum_bitcast_fusion.3) | copy-start | bytes 6291460
  249.2 7.0 %copy-start.19 = (bf16[1024,768]{0,1:T(8,128)(2,1)S(1)}, bf16[1024,768]{0,1:T(8,128)(2,1)}, u32[]{:S(2)}) copy-start(bf16[1024,768]{0,1:T(8,128)(2,1)} %fusion.13) | copy-start | bytes 4718596
  249.2 7.0 %copy-start.54 = (bf16[1,768,1,128]{3,1,0,2:T(8,128)(2,1)S(1)}, bf16[1,768,1,128]{3,1,0,2:T(8,128)(2,1)}, u32[]{:S(2)}) copy-start(bf16[1,768,1,128]{3,1,0,2:T(8,128)(2,1)} %copy-done.53) | copy-start | bytes 589828
  250.7 185.3 %collective-permute-start.2 = (bf16[2,1024,2,128]{3,1,2,0:T(8,128)(2,1)}, bf16[2,1024,2,128]{3,1,2,0:T(8,128)(2,1)}, u32[]{:S(2)}, u32[]{:S(2)}) collective-permute-start(bf16[2,1024,2,128]{3,1,2,0:T(8,128)(2,1)} %fusion.115), channel_id=1, source_target_pairs={{0,16},{16,32},{32,48},{48,64},{64,80},{80,96},{96,112},{1,17},{17... | collective-permute-start | bytes 3145736 | tf_op jit(solution)/shard_map/ppermute | solution.py:17
  260.9 3.9 copy-start.6
  292.5 6.1 %copy-start.22 = (bf16[1024,768]{0,1:T(8,128)(2,1)}, bf16[1024,768]{0,1:T(8,128)(2,1)S(1)}, u32[]{:S(2)}) copy-start(bf16[1024,768]{0,1:T(8,128)(2,1)S(1)} %fusion.14) | copy-start | bytes 4718596
  294.2 5.7 copy-start
  294.3 3.0 copy-start.42
  302.7 4.8 copy-start.11
  302.9 3.3 copy-start.12
  304.0 2.9 copy-start.21
  304.0 2.9 copy-start.37
  304.0 132.0 %collective-permute-start.3 = (bf16[2,1024,2,128]{3,1,2,0:T(8,128)(2,1)}, bf16[2,1024,2,128]{3,1,2,0:T(8,128)(2,1)}, u32[]{:S(2)}, u32[]{:S(2)}) collective-permute-start(bf16[2,1024,2,128]{3,1,2,0:T(8,128)(2,1)} %fusion.29), channel_id=1, source_target_pairs={{16,0},{32,16},{48,32},{64,48},{80,64},{96,80},{112,96},{17,1},{33... | collective-permute-start | bytes 3145736 | tf_op jit(solution)/shard_map/ppermute | solution.py:20
  317.9 16.9 %copy-start.49 = (f32[1024,128]{1,0:T(8,128)S(1)}, f32[1024,128]{1,0:T(8,128)}, u32[]{:S(2)}) copy-start(f32[1024,128]{1,0:T(8,128)} %fusion.111) | copy-start | bytes 1572868
  318.9 106.6 %all-to-all-start.3 = ((bf16[2048,2,128]{2,1,0:T(2,128)(2,1)}), bf16[2048,2,128]{2,1,0:T(2,128)(2,1)}, u32[]{:S(2)}, u32[]{:S(2)}) async-start(bf16[2048,2,128]{2,1,0:T(2,128)(2,1)} %copy.48), calls=%async_computation.3 | async-start | bytes 2097152 | tf_op jit(solution)/shard_map/all_to_all | solution.py:213
  334.8 3.7 copy-start.23
  334.8 3.7 copy-start.52
  334.8 4.3 copy-start.1
  340.5 81.4 %copy-start.66 = (pred[768]{0:T(1024)(128)(4,1)S(1)}, pred[768]{0:T(1024)(128)(4,1)}, u32[]{:S(2)}) copy-start(pred[768]{0:T(1024)(128)(4,1)} %copy-done.65) | copy-start | bytes 2308
  423.2 12.9 %copy-start.9 = (f32[1,2048,2,128]{3,1,2,0:T(8,128)S(1)}, f32[1,2048,2,128]{3,1,2,0:T(8,128)}, u32[]{:S(2)}) copy-start(f32[1,2048,2,128]{3,1,2,0:T(8,128)} %copy-done.8) | copy-start | bytes 6291460
  425.6 111.7 %all-to-all-start.5 = ((bf16[2048,2,128]{2,1,0:T(2,128)(2,1)}), bf16[2048,2,128]{2,1,0:T(2,128)(2,1)S(1)}, u32[]{:S(2)}, u32[]{:S(2)}) async-start(bf16[2048,2,128]{2,1,0:T(2,128)(2,1)} %copy.52), calls=%async_computation.5 | async-start | bytes 2097152 | tf_op jit(solution)/shard_map/all_to_all | solution.py:214
  439.4 16.2 %copy-start.24 = (f32[768,2,2,128]{3,2,1,0:T(2,128)S(1)}, f32[768,2,2,128]{3,2,1,0:T(2,128)}, u32[]{:S(2)}) copy-start(f32[768,2,2,128]{3,2,1,0:T(2,128)} %copy.55) | copy-start | bytes 4718596
  439.4 16.2 %copy-start.64 = (s32[768]{0:T(1024)S(1)}, s32[768]{0:T(1024)}, u32[]{:S(2)}) copy-start(s32[768]{0:T(1024)} %copy-done.63) | copy-start | bytes 9220
  558.2 20.5 %all-to-all-start.6 = ((bf16[2048,2,128]{2,1,0:T(2,128)(2,1)}), bf16[2048,2,128]{2,1,0:T(2,128)(2,1)S(1)}, u32[]{:S(2)}, u32[]{:S(2)}) async-start(bf16[2048,2,128]{2,1,0:T(2,128)(2,1)} %get-tuple-element.15), calls=%async_computation.6 | async-start | bytes 2097152 | tf_op jit(solution)/shard_map/all_to_all | solution.py:215
  (34 other events, 55.8 us)
Sparse Core Ops, SparseCore 0:
  106.2 87.8 all-reduce.2
  319.1 102.7 all-reduce.4
where the time goes:
time: 599 us; the launch traced here: 588 us
  waiting for transfers between devices  199 us (33%)
  other arithmetic  105 us (18%)
  local copies, waits for them, and re-layouts  96.1 us (16%)
  matrix products  87 us (15%)
  starting transfers between devices  63.8 us (11%)
  blocking collectives  20.9 us (3%)
  between operations  15.7 us (3%)
    psum x1, waiting for transfers between devices, shards(): glob_pair = lax.psum(picked.astype(jnp.bfloat16), 'ctx')  80.7 us
    scatter-add x1, other arithmetic, shards(): grad_pair.at[:, row_index]  75.7 us
    psum x1, waiting for transfers between devices, shards(): lax.psum(glob_grad.astype(jnp.bfloat16), 'ctx').astype(jnp.float32)  71.8 us
    dot_general x16, matrix products, rows_by_cols(): lax.dot_general(left, right, (((1,), (1,)), ((), ())), preferred_element_...  36.7 us
    dot_general x16, matrix products, cols_by_rows(): lax.dot_general(left, right, (((0,), (0,)), ((), ())), preferred_element_...  22.7 us
    all_to_all x1, blocking collectives, shards(): lax.all_to_all(grad_pair[1], 'head', split_axis=0, concat_axis=1, tiled=T...  20.9 us
    another operation x1, local copies, waits for them, and re-layouts, shards(): pair = jnp.stack([k_local, v_local])  18.1 us
    concatenate x1, local copies, waits for them, and re-layouts, shards(): grad_pair = jnp.concatenate([grad_first, grad_second], axis=1)  16.1 us
  transfers between devices with their start and end apart: 13, of which 6 were waited for; matrix products, arithmetic and copies ran while one was open for 41% of the time, Pallas kernels for 0%

commit v1 on v0

v1 whole, which is shorter than its diff:
```python
import functools

import jax
import jax.numpy as jnp
from jax import lax
from jax.experimental import pallas as pl
from jax.experimental.pallas import tpu as pltpu
from jax.sharding import Mesh, PartitionSpec as P

BLK = 128
HD = 128
WIN = 8
HALO = WIN - 1
RUN = 16
EXT = HALO + RUN
GLOB = 6
BAND = WIN + 1
NEG = -1e30
SCALE = HD ** -0.5
LOG2E = 1.4426950408889634
GROUP = ("xh", "xl", "z", "c")
F32 = jnp.float32
BF16 = jnp.bfloat16


def dot(a, b):
    return jnp.dot(a, b, preferred_element_type=F32)


def attention_kernel(
    info, kv, qd, halo_a, halo_b, glob,
    odq, own, back_a, back_b, glob_grad,
    kx, vx, kt, vt, kgt, vgt, dk, dv, dkg, dvg, st, pb, ds,
):
    w = info[0]
    last_y = info[1]
    for h in range(HALO):
        kx[0, h] = halo_a[h, 0]
        vx[0, h] = halo_a[h, 1]
        kx[1, h] = halo_b[h, 0]
        vx[1, h] = halo_b[h, 1]

    @pl.when(last_y == 1)
    def _():
        for h in range(HALO):
            kx[1, h] = kv[17 + h, 0]
            vx[1, h] = kv[17 + h, 1]

    for t in range(RUN):
        p0 = (t // 8) * 16 + t % 8
        p1 = (1 - t // 8) * 16 + 8 + t % 8
        kx[0, HALO + t] = kv[p0, 0]
        vx[0, HALO + t] = kv[p0, 1]
        kx[1, HALO + t] = kv[p1, 0]
        vx[1, HALO + t] = kv[p1, 1]
    for e in range(EXT):
        for ch in range(2):
            kt[ch, :, e * BLK:(e + 1) * BLK] = kx[ch, e].T
            vt[ch, :, e * BLK:(e + 1) * BLK] = vx[ch, e].T
    for s in range(GLOB):
        kgt[:, s * BLK:(s + 1) * BLK] = glob[s, 0].T
        vgt[:, s * BLK:(s + 1) * BLK] = glob[s, 1].T
    dk[...] = jnp.zeros_like(dk)
    dv[...] = jnp.zeros_like(dv)
    dkg[...] = jnp.zeros_like(dkg)
    dvg[...] = jnp.zeros_like(dvg)

    lane = lax.broadcasted_iota(jnp.int32, (1, 2 * BLK), 1)
    upper = lane // BLK
    lane_full = lax.broadcasted_iota(jnp.int32, (BLK, 2 * BLK), 1)
    row_full = lax.broadcasted_iota(jnp.int32, (BLK, 2 * BLK), 0)
    c = SCALE * LOG2E

    def tile(ch, tt):
        t0 = 2 * tt
        seg = tt // 4
        if ch == 0:
            pos = seg * 16 + t0 - seg * 8
        else:
            pos = (1 - seg) * 16 + 8 + t0 - seg * 8
        base = info[2 + ch]
        first = base + t0
        q = qd[pl.ds(pos, 2), 0].reshape(2 * BLK, HD)
        do = qd[pl.ds(pos, 2), 1].reshape(2 * BLK, HD)
        qt = q.T
        dot_ = do.T
        top = None
        for r in range(BAND):
            s = dot(kx[ch, t0 + r], qt)
            if r >= BAND - 2:
                s = jnp.where(row_full <= lane_full - BLK * (r - HALO), s, NEG)
            dist = HALO - r + upper
            ok = jnp.logical_and(dist < w, first - HALO + r >= 0)
            s = jnp.where(ok, s, NEG)
            st[r * BLK:(r + 1) * BLK] = s
            here = jnp.max(s.reshape(BLK // 8, 8, 2 * BLK), axis=0)
            top = here if top is None else jnp.maximum(top, here)
        for g in range(GLOB):
            s = dot(glob[g, 0], qt)
            ok = info[4 + g] <= first + upper - w
            s = jnp.where(ok, s, NEG)
            st[(BAND + g) * BLK:(BAND + g + 1) * BLK] = s
            top = jnp.maximum(top, jnp.max(s.reshape(BLK // 8, 8, 2 * BLK), axis=0))
        top = jnp.max(top, axis=0, keepdims=True) * c
        total = None
        for r in range(BAND + GLOB):
            rows = slice(r * BLK, (r + 1) * BLK)
            e = jnp.exp2(st[rows] * c - top)
            st[rows] = e
            here = jnp.sum(e.reshape(BLK // 8, 8, 2 * BLK), axis=0)
            total = here if total is None else total + here
        inv = 1.0 / jnp.sum(total, axis=0, keepdims=True)
        for r in range(BAND + GLOB):
            rows = slice(r * BLK, (r + 1) * BLK)
            e = st[rows] * inv
            st[rows] = e
            pb[rows] = e.astype(BF16)
        cut = BAND * BLK
        cols = pl.ds(pl.multiple_of(t0 * BLK, 2 * BLK), cut)
        ot = dot(vt[ch, :, cols], pb[:cut]) + dot(vgt[...], pb[cut:])
        ob = ot.astype(BF16)
        delta = jnp.sum(ob.astype(F32) * dot_.astype(F32), axis=0, keepdims=True)
        odq[pl.ds(pos, 2), 0] = ob.T.reshape(2, BLK, HD)
        for r in range(BAND + GLOB):
            rows = slice(r * BLK, (r + 1) * BLK)
            v = vx[ch, t0 + r] if r < BAND else glob[r - BAND, 1]
            g = (st[rows] * (dot(v, dot_) - delta)).astype(BF16)
            ds[rows] = g
            if r < BAND:
                dk[ch, t0 + r] += dot(g, q)
                dv[ch, t0 + r] += dot(pb[rows], do)
            else:
                dkg[r - BAND] += dot(g, q)
                dvg[r - BAND] += dot(pb[rows], do)
        dqt = (dot(kt[ch, :, cols], ds[:cut]) + dot(kgt[...], ds[cut:])) * SCALE
        odq[pl.ds(pos, 2), 1] = dqt.astype(BF16).T.reshape(2, BLK, HD)

    def step(tt, carry):
        tile(0, tt)
        tile(1, tt)
        return carry

    lax.fori_loop(0, RUN // 2, step, 0)

    for t in range(RUN):
        p0 = (t // 8) * 16 + t % 8
        p1 = (1 - t // 8) * 16 + 8 + t % 8
        own[p0, 0] = dk[0, HALO + t] * SCALE
        own[p0, 1] = dv[0, HALO + t]
        own[p1, 0] = dk[1, HALO + t] * SCALE
        own[p1, 1] = dv[1, HALO + t]

    @pl.when(last_y == 1)
    def _():
        for h in range(HALO):
            own[17 + h, 0] += dk[1, h] * SCALE
            own[17 + h, 1] += dv[1, h]

    for h in range(HALO):
        back_a[h, 0] = (dk[0, h] * SCALE).astype(BF16)
        back_a[h, 1] = dv[0, h].astype(BF16)
        back_b[h, 0] = (dk[1, h] * SCALE).astype(BF16)
        back_b[h, 1] = dv[1, h].astype(BF16)
    for g in range(GLOB):
        glob_grad[g, 0] = (dkg[g] * SCALE).astype(BF16)
        glob_grad[g, 1] = dvg[g].astype(BF16)


def vmem():
    return pl.BlockSpec(memory_space=pltpu.VMEM)


def attention(info, kv, qd, halo_a, halo_b, glob):
    sds = jax.ShapeDtypeStruct
    return pl.pallas_call(
        attention_kernel,
        out_shape=(
            sds((32, 2, BLK, HD), BF16),
            sds((32, 2, BLK, HD), F32),
            sds((HALO, 2, BLK, HD), BF16),
            sds((HALO, 2, BLK, HD), BF16),
            sds((GLOB, 2, BLK, HD), BF16),
        ),
        in_specs=[pl.BlockSpec(memory_space=pltpu.SMEM)] + [vmem()] * 5,
        out_specs=(vmem(),) * 5,
        scratch_shapes=[
            pltpu.VMEM((2, EXT, BLK, HD), BF16),
            pltpu.VMEM((2, EXT, BLK, HD), BF16),
            pltpu.VMEM((2, HD, EXT * BLK + BLK), BF16),
            pltpu.VMEM((2, HD, EXT * BLK + BLK), BF16),
            pltpu.VMEM((HD, GLOB * BLK), BF16),
            pltpu.VMEM((HD, GLOB * BLK), BF16),
            pltpu.VMEM((2, EXT, BLK, HD), F32),
            pltpu.VMEM((2, EXT, BLK, HD), F32),
            pltpu.VMEM((GLOB, BLK, HD), F32),
            pltpu.VMEM((GLOB, BLK, HD), F32),
            pltpu.VMEM(((BAND + GLOB) * BLK, 2 * BLK), F32),
            pltpu.VMEM(((BAND + GLOB) * BLK, 2 * BLK), BF16),
            pltpu.VMEM(((BAND + GLOB) * BLK, 2 * BLK), BF16),
        ],
        compiler_params=pltpu.CompilerParams(vmem_limit_bytes=52 * 2**20),
        cost_estimate=pl.CostEstimate(
            flops=12 * 448 * BLK**3, bytes_accessed=16 * 2**20, transcendentals=448 * BLK * BLK
        ),
        name="attention",
    )(info, kv, qd, halo_a, halo_b, glob)


def finish_kernel(info, own, back_a, back_b, glob_one, glob_two, out):
    for p in range(32):
        for a in range(2):
            g = own[p, a]
            if 17 <= p < 24:
                g = g + back_a[p - 17, a].astype(F32)
            if 9 <= p < 16:
                g = g + back_b[p - 9, a].astype(F32)
            own_p = g
            out[p, a] = own_p.astype(BF16)
    for s in range(GLOB):
        @pl.when(info[16 + s] == 1)
        def _(s=s):
            p = info[10 + s]
            for a in range(2):
                g = own[p, a] + glob_one[s, a].astype(F32) + glob_two[s, a].astype(F32)
                ia = jnp.clip(p - 17, 0, HALO - 1)
                ib = jnp.clip(p - 9, 0, HALO - 1)
                in_a = jnp.logical_and(p >= 17, p < 24)
                in_b = jnp.logical_and(p >= 9, p < 16)
                g = g + jnp.where(in_a, back_a[ia, a].astype(F32), 0.0)
                g = g + jnp.where(in_b, back_b[ib, a].astype(F32), 0.0)
                out[p, a] = g.astype(BF16)


def finish(info, own, back_a, back_b, glob_one, glob_two):
    return pl.pallas_call(
        finish_kernel,
        out_shape=jax.ShapeDtypeStruct((32, 2, BLK, HD), BF16),
        in_specs=[pl.BlockSpec(memory_space=pltpu.SMEM)] + [vmem()] * 5,
        out_specs=vmem(),
        compiler_params=pltpu.CompilerParams(vmem_limit_bytes=24 * 2**20),
        cost_estimate=pl.CostEstimate(flops=2**21, bytes_accessed=8 * 2**20, transcendentals=0),
        name="finish",
    )(info, own, back_a, back_b, glob_one, glob_two)


def to_heads(x, y):
    pair = jnp.stack([x, y], axis=0).reshape(2, BLK, 16, 2, HD)
    pair = jnp.transpose(pair, (3, 2, 0, 1, 4)).reshape(32, 2, BLK, HD)
    return pair


def to_rows(pair):
    pair = pair.reshape(2, 16, 2, BLK, HD)
    pair = jnp.transpose(pair, (2, 3, 1, 0, 4)).reshape(2, BLK, 32, HD)
    return pair[0], pair[1]


def exchange(x):
    return lax.all_to_all(x, GROUP, 0, 0, tiled=True)


PAIR_ONE = [(0, 1), (1, 0), (2, 3), (3, 2)]
PAIR_TWO = [(1, 2), (2, 1), (3, 0), (0, 3)]


def shards(query, keys, values, grad_out, window, global_blocks):
    me = lax.axis_index("y")
    w = jnp.where(lax.axis_index("xh") == 0, window[0], window[1])
    low = global_blocks < 64
    owner = jnp.where(low, global_blocks // RUN, (127 - global_blocks) // RUN)
    t = global_blocks % RUN
    where = jnp.where(low, (t // 8) * 16 + t % 8, (1 - t // 8) * 16 + 8 + t % 8)
    info = jnp.concatenate([
        jnp.stack([w, (me == 3).astype(jnp.int32), RUN * me, 112 - RUN * me]),
        global_blocks, where, (owner == me).astype(jnp.int32),
    ]).astype(jnp.int32)

    kv = exchange(to_heads(keys, values))
    qd = exchange(to_heads(query, grad_out))

    halo_a = lax.ppermute(kv[17:24], "y", [(0, 1), (1, 2), (2, 3)])
    halo_b = lax.ppermute(kv[9:16], "y", [(3, 2), (2, 1), (1, 0)])
    mine = jnp.concatenate([lax.dynamic_slice_in_dim(kv, where[s], 1, 0) for s in range(GLOB)], axis=0)
    other = lax.ppermute(mine, "y", PAIR_ONE)
    mine = jnp.where((owner == me)[:, None, None, None], mine, other)
    other = lax.ppermute(mine, "y", PAIR_TWO)
    glob = jnp.where((owner // 2 == me // 2)[:, None, None, None], mine, other)

    odq, own, back_a, back_b, glob_grad = attention(info, kv, qd, halo_a, halo_b, glob)

    odq = exchange(odq)
    back_a = lax.ppermute(back_a, "y", [(1, 0), (2, 1), (3, 2)])
    back_b = lax.ppermute(back_b, "y", [(0, 1), (1, 2), (2, 3)])
    other = lax.ppermute(glob_grad, "y", PAIR_ONE)
    glob_grad = (glob_grad.astype(F32) + other.astype(F32)).astype(BF16)
    other = lax.ppermute(glob_grad, "y", PAIR_TWO)
    dkv = exchange(finish(info, own, back_a, back_b, glob_grad, other))
    attended, grad_query = to_rows(odq)
    grad_keys, grad_values = to_rows(dkv)
    return attended, grad_query, grad_keys, grad_values


def solution(mesh):
    fine = Mesh(mesh.devices.reshape(4, 2, 2, 4, 2), ("y", "xh", "xl", "z", "c"))
    rows = P(("y", "xh", "xl", "z", "c"), None, None)
    return jax.shard_map(
        shards,
        mesh=fine,
        in_specs=(rows, rows, rows, rows, P(("xl", "z", "c")), P()),
        out_specs=(rows,) * 4,
        check_vma=False,
    )
```

time: 599 us -> 226 us (0.38); the launches traced: 588 us -> 224 us
  waiting for transfers between devices: 199 us -> 59.8 us
  other arithmetic: 105 us -> 5.62 us
  matrix products: 87 us -> 0 us
  local copies, waits for them, and re-layouts: 96.1 us -> 20.9 us
  Pallas kernels: 0 us -> 71.2 us
  blocking collectives: 20.9 us -> 0 us
  starting transfers between devices: 63.8 us -> 52.9 us
    psum x2 -> x0, waiting for transfers between devices: 153 us -> none  [the longest x1 80.7 us: shards(): glob_pair = lax.psum(picked.astype(jnp.bfloat16), 'ctx')]
    dot_general x48 -> x0, matrix products: 87 us -> none  [the longest x16 36.7 us: rows_by_cols(): lax.dot_general(left, right, (((1,), (1,)), ((), ())), preferred_element_...]
    scatter-add x1 -> x0, other arithmetic: 75.7 us -> none  [shards(): grad_pair.at[:, row_index]]
    pallas_call x0 -> x2, Pallas kernels: none -> 71.2 us  [the longest x1 68.7 us: attention(): pl.pallas_call(attention_kernel, out_shape=(sds((32, 2, BLK, HD), BF16),...]
    concatenate x3 -> x2, local copies, waits for them, and re-layouts: 35.1 us -> 0.1 us  [the longest x1 0.08 us: shards(): jnp.concatenate([jnp.stack([w, (me == 3).astype(jnp.int32), RUN * me, 112...]
    ppermute x4 -> x8, waiting for transfers between devices: 0.01 us -> 22.7 us  [the longest x1 9.04 us: shards(): other = lax.ppermute(mine, 'y', PAIR_ONE)]
    all_to_all x7 -> x4, starting transfers between devices: 53 us -> 31.4 us  [exchange(): return lax.all_to_all(x, GROUP, 0, 0, tiled=True)]
    all_to_all x1 -> x0, blocking collectives: 20.9 us -> none  [shards(): lax.all_to_all(grad_pair[1], 'head', split_axis=0, concat_axis=1, tiled=T...]
  transfers between devices with their start and end apart: 13 -> 12, of which waited for: 6 -> 7; matrix products, arithmetic and copies ran while one was open for 41% -> 7% of each run, Pallas kernels for 0% -> 1%
where the time goes in v1:
time: 226 us; the launch traced here: 224 us
  Pallas kernels  71.2 us (32%)
  waiting for transfers between devices  59.8 us (26%)
  starting transfers between devices  52.9 us (23%)
  local copies, waits for them, and re-layouts  20.9 us (9%)
  between operations  13.8 us (6%)
  other arithmetic  5.62 us (2%)
    pallas_call x1, Pallas kernels, attention(): pl.pallas_call(attention_kernel, out_shape=(sds((32, 2, BLK, HD), BF16),...  68.7 us
    all_to_all x4, waiting for transfers between devices, exchange(): return lax.all_to_all(x, GROUP, 0, 0, tiled=True)  37.1 us
    all_to_all x4, starting transfers between devices, exchange(): return lax.all_to_all(x, GROUP, 0, 0, tiled=True)  31.4 us
    slice x6, local copies, waits for them, and re-layouts, to_rows(): return (pair[0], pair[1])  10 us
    ppermute x1, waiting for transfers between devices, shards(): other = lax.ppermute(mine, 'y', PAIR_ONE)  9.04 us
    ppermute x1, waiting for transfers between devices, shards(): back_a = lax.ppermute(back_a, 'y', [(1, 0), (2, 1), (3, 2)])  8.41 us
    another operation x4, local copies, waits for them, and re-layouts, to_heads(): pair = jnp.stack([x, y], axis=0).reshape(2, BLK, 16, 2, HD)  6.37 us
    ppermute x1, starting transfers between devices, shards(): halo_a = lax.ppermute(kv[17:24], 'y', [(0, 1), (1, 2), (2, 3)])  4.77 us
  transfers between devices with their start and end apart: 12, of which 7 were waited for; matrix products, arithmetic and copies ran while one was open for 7% of the time, Pallas kernels for 1%

profile of v1, /device:TPU:1, one launch (start us, length us, event | category | flops | bytes accessed | tf_op | source)
XLA Modules:
  0.0 224.2 jit_solution(4669597102113506253)
XLA Ops:
  0.6 1.7 copy.10
  2.4 0.4 copy.11
  2.8 1.5 pad_maximum_fusion
  4.3 9.6 %all-to-all-start = ((bf16[32,2,128,128]{3,2,1,0:T(8,128)(2,1)}), bf16[32,2,128,128]{3,2,1,0:T(8,128)(2,1)S(1)}, u32[]{:S(2)}, u32[]{:S(2)}) async-start(bf16[32,2,128,128]{3,2,1,0:T(8,128)(2,1)} %bitcast.9), calls=%async_computation | async-start | bytes 4194304 | tf_op jit(solution)/shard_map/all_to_all | solution.py:259
  13.9 0.6 fusion.5
  22.3 1.6 copy.12
  23.9 2.6 %copy.13 = bf16[1,128,16,2,128]{4,1,0,2,3:T(8,128)(2,1)} copy(bf16[1,128,16,2,128]{4,3,2,1,0:T(2,128)(2,1)} %bitcast.36) | data formatting | bytes 2097152 | tf_op jit(solution)/shard_map/stack | solution.py:247
  30.4 2.8 %pad_maximum_fusion.1 = bf16[2,128,16,2,128]{4,1,0,2,3:T(8,128)(2,1)} fusion(bf16[1,128,16,2,128]{4,1,0,2,3:T(8,128)(2,1)} %copy.13, bf16[1,128,16,2,128]{4,1,0,2,3:T(8,128)(2,1)S(1)} %copy.12), kind=kLoop, calls=%fused_computation.1 | loop fusion | flops 1048576 | bytes 4194304 | tf_op jit(solution)/shard_map/stack | solution.py:247
  33.2 9.0 %all-to-all-done.kv = bf16[32,2,128,128]{3,2,1,0:T(8,128)(2,1)S(1)} async-done(((bf16[32,2,128,128]{3,2,1,0:T(8,128)(2,1)}), bf16[32,2,128,128]{3,2,1,0:T(8,128)(2,1)S(1)}, u32[]{:S(2)}, u32[]{:S(2)}) %all-to-all-start) | async-done | bytes 2097184 | tf_op jit(solution)/shard_map/all_to_all | solution.py:259
  42.2 5.2 %all-to-all-start.1 = ((bf16[32,2,128,128]{3,2,1,0:T(8,128)(2,1)}), bf16[32,2,128,128]{3,2,1,0:T(8,128)(2,1)}, u32[]{:S(2)}, u32[]{:S(2)}) async-start(bf16[32,2,128,128]{3,2,1,0:T(8,128)(2,1)} %bitcast.13), calls=%async_computation.1 | async-start | bytes 4194304 | tf_op jit(solution)/shard_map/all_to_all | solution.py:259
  47.4 0.0 copy-start.3
  47.5 1.4 collective-permute-start.2
  48.9 9.0 %collective-permute-done.2 = bf16[6,2,128,128]{3,2,1,0:T(8,128)(2,1)S(1)} collective-permute-done((bf16[6,2,128,128]{3,2,1,0:T(8,128)(2,1)S(1)}, bf16[6,2,128,128]{3,2,1,0:T(8,128)(2,1)S(1)}, u32[]{:S(2)}, u32[]{:S(2)}) %collective-permute-start.2) | collective-permute-done | bytes 393248 | tf_op jit(solution)/shard_map/ppermute | solution.py:284
  58.0 0.1 broadcast_select_fusion
  58.1 2.8 %collective-permute-start.3 = (bf16[6,2,128,128]{3,2,1,0:T(8,128)(2,1)S(1)}, bf16[6,2,128,128]{3,2,1,0:T(8,128)(2,1)}, u32[]{:S(2)}, u32[]{:S(2)}) collective-permute-start(bf16[6,2,128,128]{3,2,1,0:T(8,128)(2,1)S(1)} %broadcast_select_fusion), channel_id=1, source_target_pairs={{32,64},{64,32},{96,0},{0,96},{33,65},{65,33},{97,1},{1,97},{34,66... | collective-permute-start | bytes 1179656 | tf_op jit(solution)/shard_map/ppermute | solution.py:286
  60.9 0.1 fusion.4
  61.0 1.3 collective-permute-start.1
  62.3 4.8 %collective-permute-start = (bf16[7,2,128,128]{3,2,1,0:T(8,128)(2,1)S(1)}, bf16[7,2,128,128]{3,2,1,0:T(8,128)(2,1)}, u32[]{:S(2)}, u32[]{:S(2)}) collective-permute-start(bf16[7,2,128,128]{3,2,1,0:T(8,128)(2,1)S(1)} %get-tuple-element.23), channel_id=1, source_target_pairs={{0,32},{32,64},{64,96},{1,33},{33,65},{65,97},{2,34},{34,66},{66,9... | collective-permute-start | bytes 1376264 | tf_op jit(solution)/shard_map/ppermute | solution.py:281
  67.1 0.6 fusion.6
  69.0 0.1 concatenate.8.info
  69.0 0.0 collective-permute-done.3
  69.1 1.1 broadcast_select_fusion.1.glob
  70.2 5.6 %all-to-all-done.1.qd = bf16[32,2,128,128]{3,2,1,0:T(8,128)(2,1)} async-done(((bf16[32,2,128,128]{3,2,1,0:T(8,128)(2,1)}), bf16[32,2,128,128]{3,2,1,0:T(8,128)(2,1)}, u32[]{:S(2)}, u32[]{:S(2)}) %all-to-all-start.1) | async-done | bytes 2097184 | tf_op jit(solution)/shard_map/all_to_all | solution.py:259
  75.8 0.0 collective-permute-done.1.halo_b
  75.8 0.8 copy-done.5
  76.6 0.0 collective-permute-done.halo_a
  76.6 68.7 %attention.1 = (bf16[32,2,128,128]{3,2,1,0:T(8,128)(2,1)}, f32[32,2,128,128]{3,2,1,0:T(8,128)}, bf16[7,2,128,128]{3,2,1,0:T(8,128)(2,1)S(1)}, bf16[7,2,128,128]{...) custom-call(s32[22]{0:T(128)S(1)} %concatenate.8.info, bf16[32,2,128,128]{3,2,1,0:T(8,128)(2,1)} %copy-done.1, ...), custom_call_target="tpu_custom_call" | custom-call | flops 11274289152 | bytes 16777216 | tf_op jit(solution)/shard_map/attention/pallas_call | solution.py:175
  145.3 7.7 %all-to-all-start.2 = ((bf16[32,2,128,128]{3,2,1,0:T(8,128)(2,1)}), bf16[32,2,128,128]{3,2,1,0:T(8,128)(2,1)}, u32[]{:S(2)}, u32[]{:S(2)}) async-start(bf16[32,2,128,128]{3,2,1,0:T(8,128)(2,1)} %get-tuple-element.9), calls=%async_computation.2 | async-start | bytes 4194304 | tf_op jit(solution)/shard_map/all_to_all | solution.py:259
  153.0 4.7 %collective-permute-start.6 = (bf16[6,2,128,128]{3,2,1,0:T(8,128)(2,1)S(1)}, bf16[6,2,128,128]{3,2,1,0:T(8,128)(2,1)S(1)}, u32[]{:S(2)}, u32[]{:S(2)}) collective-permute-start(bf16[6,2,128,128]{3,2,1,0:T(8,128)(2,1)S(1)} %get-tuple-element.13), channel_id=1, source_target_pairs={{0,32},{32,0},{64,96},{96,64},{1,33},{33,1},{65,97},{97,65},{2,34}... | collective-permute-start | bytes 1179656 | tf_op jit(solution)/shard_map/ppermute | solution.py:294
  157.7 1.3 collective-permute-start.4
  159.0 4.0 %collective-permute-start.5 = (bf16[7,2,128,128]{3,2,1,0:T(8,128)(2,1)S(1)}, bf16[7,2,128,128]{3,2,1,0:T(8,128)(2,1)S(1)}, u32[]{:S(2)}, u32[]{:S(2)}) collective-permute-start(bf16[7,2,128,128]{3,2,1,0:T(8,128)(2,1)S(1)} %get-tuple-element.12), channel_id=1, source_target_pairs={{0,32},{32,64},{64,96},{1,33},{33,65},{65,97},{2,34},{34,66},{66,9... | collective-permute-start | bytes 1376264 | tf_op jit(solution)/shard_map/ppermute | solution.py:293
  163.0 4.0 %collective-permute-done.6 = bf16[6,2,128,128]{3,2,1,0:T(8,128)(2,1)S(1)} collective-permute-done((bf16[6,2,128,128]{3,2,1,0:T(8,128)(2,1)S(1)}, bf16[6,2,128,128]{3,2,1,0:T(8,128)(2,1)S(1)}, u32[]{:S(2)}, u32[]{:S(2)}) %collective-permute-start.6) | collective-permute-done | bytes 393248 | tf_op jit(solution)/shard_map/ppermute | solution.py:294
  167.1 0.1 add_convert_fusion.glob_one
  167.2 1.3 collective-permute-start.7
  168.5 8.4 %collective-permute-done.4.back_a = bf16[7,2,128,128]{3,2,1,0:T(8,128)(2,1)S(1)} collective-permute-done((bf16[7,2,128,128]{3,2,1,0:T(8,128)(2,1)S(1)}, bf16[7,2,128,128]{3,2,1,0:T(8,128)(2,1)S(1)}, u32[]{:S(2)}, u32[]{:S(2)}) %collective-permute-start.4) | collective-permute-done | bytes 458784 | tf_op jit(solution)/shard_map/ppermute | solution.py:292
  176.9 0.0 collective-permute-done.5.back_b
  176.9 1.2 collective-permute-done.7.glob_two
  178.1 2.2 copy-done
  180.2 2.5 %finish.1 = bf16[32,2,128,128]{3,2,1,0:T(8,128)(2,1)} custom-call(s32[22]{0:T(128)S(1)} %concatenate.8.info, f32[32,2,128,128]{3,2,1,0:T(8,128)S(1)} %copy-done, bf16[7,2,128,128]{3,2,1,0:T(8,128)(2,1)S(1)} %collective-permute-done.4.back_a, bf16[7,2,128,128]{3,2,1,0:T(8,128)(2,1)S(1)} %collective-permute-done.5.back_b, ...), custom_call_target="tpu_custom_call" | custom-call | flops 2097152 | bytes 8388608 | tf_op jit(solution)/shard_map/finish/pallas_call | solution.py:235
  182.7 0.0 all-to-all-done.2
  182.7 8.9 %all-to-all-start.3 = ((bf16[32,2,128,128]{3,2,1,0:T(8,128)(2,1)}), bf16[32,2,128,128]{3,2,1,0:T(8,128)(2,1)S(1)}, u32[]{:S(2)}, u32[]{:S(2)}) async-start(bf16[32,2,128,128]{3,2,1,0:T(8,128)(2,1)} %finish.1), calls=%async_computation.3 | async-start | bytes 4194304 | tf_op jit(solution)/shard_map/all_to_all | solution.py:259
  191.6 1.7 fusion.3
  193.3 2.0 copy.15
  195.4 2.0 copy.14
  197.4 22.5 %all-to-all-done.3 = bf16[32,2,128,128]{3,2,1,0:T(8,128)(2,1)S(1)} async-done(((bf16[32,2,128,128]{3,2,1,0:T(8,128)(2,1)}), bf16[32,2,128,128]{3,2,1,0:T(8,128)(2,1)S(1)}, u32[]{:S(2)}, u32[]{:S(2)}) %all-to-all-start.3) | async-done | bytes 2097184 | tf_op jit(solution)/shard_map/all_to_all | solution.py:259
  219.9 0.1 fusion.2
  220.1 2.0 copy.17
  222.1 2.0 copy.16
  (18 shorter events, 0.2 us)
Async XLA Ops:
  0.6 1.7 copy-start.2
  4.3 9.6 %copy-start.4 = (s32[6]{0:T(128)S(1)}, s32[6]{0:T(128)}, u32[]{:S(2)}) copy-start(s32[6]{0:T(128)} %param.11) | copy-start | bytes 76
  4.3 37.9 %all-to-all-start = ((bf16[32,2,128,128]{3,2,1,0:T(8,128)(2,1)}), bf16[32,2,128,128]{3,2,1,0:T(8,128)(2,1)S(1)}, u32[]{:S(2)}, u32[]{:S(2)}) async-start(bf16[32,2,128,128]{3,2,1,0:T(8,128)(2,1)} %bitcast.9), calls=%async_computation | async-start | bytes 4194304 | tf_op jit(solution)/shard_map/all_to_all | solution.py:259
  42.2 18.8 %copy-start.1 = (bf16[32,2,128,128]{3,2,1,0:T(8,128)(2,1)}, bf16[32,2,128,128]{3,2,1,0:T(8,128)(2,1)S(1)}, u32[]{:S(2)}) copy-start(bf16[32,2,128,128]{3,2,1,0:T(8,128)(2,1)S(1)} %all-to-all-done.kv) | copy-start | bytes 6291460
  42.2 33.6 %all-to-all-start.1 = ((bf16[32,2,128,128]{3,2,1,0:T(8,128)(2,1)}), bf16[32,2,128,128]{3,2,1,0:T(8,128)(2,1)}, u32[]{:S(2)}, u32[]{:S(2)}) async-start(bf16[32,2,128,128]{3,2,1,0:T(8,128)(2,1)} %bitcast.13), calls=%async_computation.1 | async-start | bytes 4194304 | tf_op jit(solution)/shard_map/all_to_all | solution.py:259
  47.4 19.7 %copy-start.3 = (s32[2]{0:T(128)S(1)}, s32[2]{0:T(128)}, u32[]{:S(2)}) copy-start(s32[2]{0:T(128)} %param.10) | copy-start | bytes 28
  47.5 10.5 %collective-permute-start.2 = (bf16[6,2,128,128]{3,2,1,0:T(8,128)(2,1)S(1)}, bf16[6,2,128,128]{3,2,1,0:T(8,128)(2,1)S(1)}, u32[]{:S(2)}, u32[]{:S(2)}) collective-permute-start(bf16[6,2,128,128]{3,2,1,0:T(8,128)(2,1)S(1)} %dynamic-slice_dynamic-update-slice_fusion), channel_id=1, source_target_pairs={{0,32},{32,0},{64,96},{96,64},{1,33},{33,1},{65,97},{97,65},{2,34}... | collective-permute-start | bytes 1179656 | tf_op jit(solution)/shard_map/ppermute | solution.py:284
  58.1 11.0 %collective-permute-start.3 = (bf16[6,2,128,128]{3,2,1,0:T(8,128)(2,1)S(1)}, bf16[6,2,128,128]{3,2,1,0:T(8,128)(2,1)}, u32[]{:S(2)}, u32[]{:S(2)}) collective-permute-start(bf16[6,2,128,128]{3,2,1,0:T(8,128)(2,1)S(1)} %broadcast_select_fusion), channel_id=1, source_target_pairs={{32,64},{64,32},{96,0},{0,96},{33,65},{65,33},{97,1},{1,97},{34,66... | collective-permute-start | bytes 1179656 | tf_op jit(solution)/shard_map/ppermute | solution.py:286
  61.0 14.8 %collective-permute-start.1 = (bf16[7,2,128,128]{3,2,1,0:T(8,128)(2,1)S(1)}, bf16[7,2,128,128]{3,2,1,0:T(8,128)(2,1)S(1)}, u32[]{:S(2)}, u32[]{:S(2)}) collective-permute-start(bf16[7,2,128,128]{3,2,1,0:T(8,128)(2,1)S(1)} %get-tuple-element.22), channel_id=1, source_target_pairs={{96,64},{64,32},{32,0},{97,65},{65,33},{33,1},{98,66},{66,34},{34,... | collective-permute-start | bytes 1376264 | tf_op jit(solution)/shard_map/ppermute | solution.py:282
  62.3 14.3 %collective-permute-start = (bf16[7,2,128,128]{3,2,1,0:T(8,128)(2,1)S(1)}, bf16[7,2,128,128]{3,2,1,0:T(8,128)(2,1)}, u32[]{:S(2)}, u32[]{:S(2)}) collective-permute-start(bf16[7,2,128,128]{3,2,1,0:T(8,128)(2,1)S(1)} %get-tuple-element.23), channel_id=1, source_target_pairs={{0,32},{32,64},{64,96},{1,33},{33,65},{65,97},{2,34},{34,66},{66,9... | collective-permute-start | bytes 1376264 | tf_op jit(solution)/shard_map/ppermute | solution.py:281
  75.8 0.8 copy-start.5
  145.3 37.4 %all-to-all-start.2 = ((bf16[32,2,128,128]{3,2,1,0:T(8,128)(2,1)}), bf16[32,2,128,128]{3,2,1,0:T(8,128)(2,1)}, u32[]{:S(2)}, u32[]{:S(2)}) async-start(bf16[32,2,128,128]{3,2,1,0:T(8,128)(2,1)} %get-tuple-element.9), calls=%async_computation.2 | async-start | bytes 4194304 | tf_op jit(solution)/shard_map/all_to_all | solution.py:259
  153.0 14.0 %collective-permute-start.6 = (bf16[6,2,128,128]{3,2,1,0:T(8,128)(2,1)S(1)}, bf16[6,2,128,128]{3,2,1,0:T(8,128)(2,1)S(1)}, u32[]{:S(2)}, u32[]{:S(2)}) collective-permute-start(bf16[6,2,128,128]{3,2,1,0:T(8,128)(2,1)S(1)} %get-tuple-element.13), channel_id=1, source_target_pairs={{0,32},{32,0},{64,96},{96,64},{1,33},{33,1},{65,97},{97,65},{2,34}... | collective-permute-start | bytes 1179656 | tf_op jit(solution)/shard_map/ppermute | solution.py:294
  157.7 19.2 %collective-permute-start.4 = (bf16[7,2,128,128]{3,2,1,0:T(8,128)(2,1)S(1)}, bf16[7,2,128,128]{3,2,1,0:T(8,128)(2,1)S(1)}, u32[]{:S(2)}, u32[]{:S(2)}) collective-permute-start(bf16[7,2,128,128]{3,2,1,0:T(8,128)(2,1)S(1)} %get-tuple-element.11), channel_id=1, source_target_pairs={{32,0},{64,32},{96,64},{33,1},{65,33},{97,65},{34,2},{66,34},{98,6... | collective-permute-start | bytes 1376264 | tf_op jit(solution)/shard_map/ppermute | solution.py:292
  159.0 17.9 %collective-permute-start.5 = (bf16[7,2,128,128]{3,2,1,0:T(8,128)(2,1)S(1)}, bf16[7,2,128,128]{3,2,1,0:T(8,128)(2,1)S(1)}, u32[]{:S(2)}, u32[]{:S(2)}) collective-permute-start(bf16[7,2,128,128]{3,2,1,0:T(8,128)(2,1)S(1)} %get-tuple-element.12), channel_id=1, source_target_pairs={{0,32},{32,64},{64,96},{1,33},{33,65},{65,97},{2,34},{34,66},{66,9... | collective-permute-start | bytes 1376264 | tf_op jit(solution)/shard_map/ppermute | solution.py:293
  167.2 10.9 %collective-permute-start.7 = (bf16[6,2,128,128]{3,2,1,0:T(8,128)(2,1)S(1)}, bf16[6,2,128,128]{3,2,1,0:T(8,128)(2,1)S(1)}, u32[]{:S(2)}, u32[]{:S(2)}) collective-permute-start(bf16[6,2,128,128]{3,2,1,0:T(8,128)(2,1)S(1)} %add_convert_fusion.glob_one), channel_id=1, source_target_pairs={{32,64},{64,32},{96,0},{0,96},{33,65},{65,33},{97,1},{1,97},{34,66... | collective-permute-start | bytes 1179656 | tf_op jit(solution)/shard_map/ppermute | solution.py:296
  178.1 2.2 copy-start
  182.7 37.2 %all-to-all-start.3 = ((bf16[32,2,128,128]{3,2,1,0:T(8,128)(2,1)}), bf16[32,2,128,128]{3,2,1,0:T(8,128)(2,1)S(1)}, u32[]{:S(2)}, u32[]{:S(2)}) async-start(bf16[32,2,128,128]{3,2,1,0:T(8,128)(2,1)} %finish.1), calls=%async_computation.3 | async-start | bytes 4194304 | tf_op jit(solution)/shard_map/all_to_all | solution.py:259

commit v2 on v1

v2 whole, which is shorter than its diff:
```python
import functools

import jax
import jax.numpy as jnp
from jax import lax
from jax.experimental import pallas as pl
from jax.experimental.pallas import tpu as pltpu
from jax.sharding import Mesh, PartitionSpec as P

BLK = 128
HD = 128
WIN = 8
HALO = WIN - 1
RUN = 16
EXT = HALO + RUN
GLOB = 6
BAND = WIN + 1
NEG = -1e30
SCALE = HD ** -0.5
LOG2E = 1.4426950408889634
GROUP = ("xh", "xl", "z", "c")
F32 = jnp.float32
BF16 = jnp.bfloat16


def dot(a, b):
    return jnp.dot(a, b, preferred_element_type=F32)


def attention_kernel(
    info, kv, qd, halo_a, halo_b, glob,
    odq, own, back_a, back_b, glob_grad,
    kx, vx, kt, vt, kgt, vgt, qs, dos, st, pb, ds, pg, dg, dkg, dvg, tail,
):
    w = info[0]
    last_y = info[1]
    for h in range(HALO):
        kx[0, h] = halo_a[h, 0]
        vx[0, h] = halo_a[h, 1]
        kx[1, h] = halo_b[h, 0]
        vx[1, h] = halo_b[h, 1]

    @pl.when(last_y == 1)
    def _():
        for h in range(HALO):
            kx[1, h] = kv[17 + h, 0]
            vx[1, h] = kv[17 + h, 1]

    for t in range(RUN):
        for ch in range(2):
            p = place(ch, t)
            kx[ch, HALO + t] = kv[p, 0]
            vx[ch, HALO + t] = kv[p, 1]
    for e in range(EXT):
        for ch in range(2):
            kt[ch, :, e * BLK:(e + 1) * BLK] = kx[ch, e].T
            vt[ch, :, e * BLK:(e + 1) * BLK] = vx[ch, e].T
    for s in range(GLOB):
        kgt[:, s * BLK:(s + 1) * BLK] = glob[s, 0].T
        vgt[:, s * BLK:(s + 1) * BLK] = glob[s, 1].T

    upper = lax.broadcasted_iota(jnp.int32, (1, 2 * BLK), 1) // BLK
    lane_full = lax.broadcasted_iota(jnp.int32, (BLK, 2 * BLK), 1)
    row_full = lax.broadcasted_iota(jnp.int32, (BLK, 2 * BLK), 0)
    c = SCALE * LOG2E
    cut = BAND * BLK

    def tile(ch, tt, slot):
        t0 = 2 * tt
        seg = tt // 4
        if ch == 0:
            pos = seg * 16 + t0 - seg * 8
        else:
            pos = (1 - seg) * 16 + 8 + t0 - seg * 8
        first = info[2 + ch] + t0
        q = qd[pl.ds(pos, 2), 0].reshape(2 * BLK, HD)
        do = qd[pl.ds(pos, 2), 1].reshape(2 * BLK, HD)
        qt = q.T
        dot_ = do.T

        def allowed(r):
            if r < BAND:
                return jnp.logical_and(HALO - r + upper < w, first - HALO + r >= 0)
            return info[4 + r - BAND] <= first + upper - w

        def probs(r):
            if r < BAND:
                return pb.at[tt, r * BLK:(r + 1) * BLK]
            return pg.at[tt, (r - BAND) * BLK:(r - BAND + 1) * BLK]

        def grads(r):
            if r < BAND:
                return ds.at[tt, r * BLK:(r + 1) * BLK]
            return dg.at[tt, (r - BAND) * BLK:(r - BAND + 1) * BLK]

        keep = {}

        def scores(r):
            s = dot(kx[ch, t0 + r] if r < BAND else glob[r - BAND, 0], qt)
            if HALO <= r < BAND:
                s = jnp.where(row_full <= lane_full - BLK * (r - HALO), s, NEG)
            st[slot, r * BLK:(r + 1) * BLK] = s
            here = jnp.max(s.reshape(BLK // 8, 8, 2 * BLK), axis=0)
            here = jnp.where(allowed(r), here, NEG)
            keep["top"] = jnp.maximum(keep["top"], here) if r else here

        def after_scores():
            keep["top"] = jnp.max(keep["top"], axis=0, keepdims=True) * c

        def weigh(r):
            off = jnp.where(allowed(r), keep["top"], -NEG)
            e = jnp.exp2(st[slot, r * BLK:(r + 1) * BLK] * c - off)
            here = jnp.sum(e.reshape(BLK // 8, 8, 2 * BLK), axis=0)
            keep["total"] = keep["total"] + here if r else here
            probs(r)[...] = e.astype(BF16)

        cols = pl.ds(pl.multiple_of(t0 * BLK, 2 * BLK), cut)

        def attend():
            keep["inv"] = inv = 1.0 / jnp.sum(keep["total"], axis=0, keepdims=True)
            ot = (dot(vt[ch, :, cols], pb[tt]) + dot(vgt[...], pg[tt])) * inv
            ob = ot.astype(BF16)
            dof = dot_.astype(F32)
            keep["delta"] = jnp.sum(ob.astype(F32) * dof, axis=0, keepdims=True)
            odq[pl.ds(pos, 2), 0] = ob.T.reshape(2, BLK, HD)
            qs[tt] = (qt.astype(F32) * inv).astype(BF16).T
            dos[tt] = (dof * inv).astype(BF16).T

        def back(r):
            v = vx[ch, t0 + r] if r < BAND else glob[r - BAND, 1]
            g = dot(v, dot_) - keep["delta"]
            grads(r)[...] = (probs(r)[...].astype(F32) * g).astype(BF16)

        def finish_tile():
            dqt = (dot(kt[ch, :, cols], ds[tt]) + dot(kgt[...], dg[tt])) * (keep["inv"] * SCALE)
            odq[pl.ds(pos, 2), 1] = dqt.astype(BF16).T.reshape(2, BLK, HD)

        return scores, after_scores, weigh, attend, back, finish_tile

    for ch in range(2):
        def step(i, carry, ch=ch):
            many = range(BAND + GLOB)
            T = [tile(ch, 4 * i + k, k) for k in range(4)]
            S, M, W, A, B, F = [[f[j] for f in T] for j in range(6)]
            for r in many:
                S[0](r)
                S[1](r)
                S[2](r)
                S[3](r)
            M[0]()
            M[1]()
            M[2]()
            M[3]()
            for r in many:
                W[0](r)
                W[1](r)
                W[2](r)
                W[3](r)
            A[0]()
            A[1]()
            A[2]()
            A[3]()
            for r in many:
                B[0](r)
                B[1](r)
                B[2](r)
                B[3](r)
            F[0]()
            F[1]()
            F[2]()
            F[3]()
            return carry

        lax.fori_loop(0, RUN // 2 // 4, step, 0)

        for u in range((EXT + 1) // 2):
            for part, (weights, rows_of) in enumerate(((ds, qs), (pb, dos))):
                acc = [None, None]
                for tt in range(max(0, u - 4), min(RUN // 2, u + 1)):
                    r = 2 * (u - tt)
                    n = min(2, BAND - r)
                    if n == 2:
                        g = dot(weights[tt, r * BLK:(r + 2) * BLK], rows_of[tt])
                        g = [g[:BLK], g[BLK:]]
                    else:
                        g = [dot(weights[tt, r * BLK:(r + 1) * BLK], rows_of[tt])]
                    for k in range(n):
                        acc[k] = g[k] if acc[k] is None else acc[k] + g[k]
                for k in range(2):
                    e = 2 * u + k
                    if e >= EXT or acc[k] is None:
                        continue
                    g = acc[k] * SCALE if part == 0 else acc[k]
                    if ch == 0 and e >= RUN:
                        tail[e - RUN, part] = g
                    if e >= HALO:
                        own[place(ch, e - HALO), part] = g.astype(BF16)
                    elif ch == 0:
                        back_a[e, part] = g.astype(BF16)
                    else:
                        back_b[e, part] = g.astype(BF16)

                        @pl.when(last_y == 1)
                        def _(e=e, part=part, g=g):
                            own[17 + e, part] = (tail[e, part] + g).astype(BF16)
        for part, (weights, rows_of, keep) in enumerate(((dg, qs, dkg), (pg, dos, dvg))):
            acc = None
            for tt in range(RUN // 2):
                g = dot(weights[tt], rows_of[tt])
                acc = g if acc is None else acc + g
            if ch == 0:
                keep[...] = acc
            else:
                acc = acc + keep[...]
                if part == 0:
                    acc = acc * SCALE
                for s in range(GLOB):
                    glob_grad[s, part] = acc[s * BLK:(s + 1) * BLK].astype(BF16)


def place(ch, t):
    return (t // 8) * 16 + t % 8 if ch == 0 else (1 - t // 8) * 16 + 8 + t % 8


def vmem():
    return pl.BlockSpec(memory_space=pltpu.VMEM)


def attention(info, kv, qd, halo_a, halo_b, glob):
    sds = jax.ShapeDtypeStruct
    return pl.pallas_call(
        attention_kernel,
        out_shape=(
            sds((32, 2, BLK, HD), BF16),
            sds((32, 2, BLK, HD), BF16),
            sds((HALO, 2, BLK, HD), BF16),
            sds((HALO, 2, BLK, HD), BF16),
            sds((GLOB, 2, BLK, HD), BF16),
        ),
        in_specs=[pl.BlockSpec(memory_space=pltpu.SMEM)] + [vmem()] * 5,
        out_specs=(vmem(),) * 5,
        scratch_shapes=[
            pltpu.VMEM((2, EXT, BLK, HD), BF16),
            pltpu.VMEM((2, EXT, BLK, HD), BF16),
            pltpu.VMEM((2, HD, EXT * BLK + BLK), BF16),
            pltpu.VMEM((2, HD, EXT * BLK + BLK), BF16),
            pltpu.VMEM((HD, GLOB * BLK), BF16),
            pltpu.VMEM((HD, GLOB * BLK), BF16),
            pltpu.VMEM((RUN // 2, 2 * BLK, HD), BF16),
            pltpu.VMEM((RUN // 2, 2 * BLK, HD), BF16),
            pltpu.VMEM((4, (BAND + GLOB) * BLK, 2 * BLK), F32),
            pltpu.VMEM((RUN // 2, BAND * BLK, 2 * BLK), BF16),
            pltpu.VMEM((RUN // 2, BAND * BLK, 2 * BLK), BF16),
            pltpu.VMEM((RUN // 2, GLOB * BLK, 2 * BLK), BF16),
            pltpu.VMEM((RUN // 2, GLOB * BLK, 2 * BLK), BF16),
            pltpu.VMEM((GLOB * BLK, HD), F32),
            pltpu.VMEM((GLOB * BLK, HD), F32),
            pltpu.VMEM((HALO, 2, BLK, HD), F32),
        ],
        compiler_params=pltpu.CompilerParams(vmem_limit_bytes=52 * 2**20),
        cost_estimate=pl.CostEstimate(
            flops=12 * 448 * BLK**3, bytes_accessed=16 * 2**20, transcendentals=448 * BLK * BLK
        ),
        name="attention",
    )(info, kv, qd, halo_a, halo_b, glob)


def finish_kernel(info, own, back_a, back_b, glob_one, glob_two, out):
    for p in range(32):
        if 17 <= p < 24:
            out[p] = (own[p].astype(F32) + back_a[p - 17].astype(F32)).astype(BF16)
        elif 9 <= p < 16:
            out[p] = (own[p].astype(F32) + back_b[p - 9].astype(F32)).astype(BF16)
        else:
            out[p] = own[p]
    for s in range(GLOB):
        @pl.when(info[16 + s] == 1)
        def _(s=s):
            p = info[10 + s]
            ia = jnp.clip(p - 17, 0, HALO - 1)
            ib = jnp.clip(p - 9, 0, HALO - 1)
            in_a = jnp.logical_and(p >= 17, p < 24)
            in_b = jnp.logical_and(p >= 9, p < 16)
            g = own[p].astype(F32) + glob_one[s].astype(F32) + glob_two[s].astype(F32)
            g = g + jnp.where(in_a, back_a[ia].astype(F32), 0.0)
            g = g + jnp.where(in_b, back_b[ib].astype(F32), 0.0)
            out[p] = g.astype(BF16)


def finish(info, own, back_a, back_b, glob_one, glob_two):
    return pl.pallas_call(
        finish_kernel,
        out_shape=jax.ShapeDtypeStruct((32, 2, BLK, HD), BF16),
        in_specs=[pl.BlockSpec(memory_space=pltpu.SMEM)] + [vmem()] * 5,
        out_specs=vmem(),
        compiler_params=pltpu.CompilerParams(vmem_limit_bytes=16 * 2**20),
        cost_estimate=pl.CostEstimate(flops=2**21, bytes_accessed=6 * 2**20, transcendentals=0),
        name="finish",
    )(info, own, back_a, back_b, glob_one, glob_two)


def to_heads(x, y):
    pair = jnp.stack([x, y], axis=0).reshape(2, BLK, 16, 2, HD)
    pair = jnp.transpose(pair, (3, 2, 0, 1, 4)).reshape(32, 2, BLK, HD)
    return pair


def to_rows(pair):
    pair = pair.reshape(2, 16, 2, BLK, HD)
    pair = jnp.transpose(pair, (2, 3, 1, 0, 4)).reshape(2, BLK, 32, HD)
    return pair[0], pair[1]


def exchange(x):
    return lax.all_to_all(x, GROUP, 0, 0, tiled=True)


PAIR_ONE = [(0, 1), (1, 0), (2, 3), (3, 2)]
PAIR_TWO = [(1, 2), (2, 1), (3, 0), (0, 3)]


def shards(query, keys, values, grad_out, window, global_blocks):
    me = lax.axis_index("y")
    w = jnp.where(lax.axis_index("xh") == 0, window[0], window[1])
    low = global_blocks < 64
    owner = jnp.where(low, global_blocks // RUN, (127 - global_blocks) // RUN)
    t = global_blocks % RUN
    where = jnp.where(low, (t // 8) * 16 + t % 8, (1 - t // 8) * 16 + 8 + t % 8)
    info = jnp.concatenate([
        jnp.stack([w, (me == 3).astype(jnp.int32), RUN * me, 112 - RUN * me]),
        global_blocks, where, (owner == me).astype(jnp.int32),
    ]).astype(jnp.int32)

    kv = exchange(to_heads(keys, values))
    qd = exchange(to_heads(query, grad_out))

    halo_a = lax.ppermute(kv[17:24], "y", [(0, 1), (1, 2), (2, 3)])
    halo_b = lax.ppermute(kv[9:16], "y", [(3, 2), (2, 1), (1, 0)])
    mine = jnp.concatenate([lax.dynamic_slice_in_dim(kv, where[s], 1, 0) for s in range(GLOB)], axis=0)
    other = lax.ppermute(mine, "y", PAIR_ONE)
    mine = jnp.where((owner == me)[:, None, None, None], mine, other)
    other = lax.ppermute(mine, "y", PAIR_TWO)
    glob = jnp.where((owner // 2 == me // 2)[:, None, None, None], mine, other)

    odq, own, back_a, back_b, glob_grad = attention(info, kv, qd, halo_a, halo_b, glob)

    odq = exchange(odq)
    back_a = lax.ppermute(back_a, "y", [(1, 0), (2, 1), (3, 2)])
    back_b = lax.ppermute(back_b, "y", [(0, 1), (1, 2), (2, 3)])
    other = lax.ppermute(glob_grad, "y", PAIR_ONE)
    glob_grad = (glob_grad.astype(F32) + other.astype(F32)).astype(BF16)
    other = lax.ppermute(glob_grad, "y", PAIR_TWO)
    dkv = exchange(finish(info, own, back_a, back_b, glob_grad, other))
    attended, grad_query = to_rows(odq)
    grad_keys, grad_values = to_rows(dkv)
    return attended, grad_query, grad_keys, grad_values


def solution(mesh):
    fine = Mesh(mesh.devices.reshape(4, 2, 2, 4, 2), ("y", "xh", "xl", "z", "c"))
    rows = P(("y", "xh", "xl", "z", "c"), None, None)
    return jax.shard_map(
        shards,
        mesh=fine,
        in_specs=(rows, rows, rows, rows, P(("xl", "z", "c")), P()),
        out_specs=(rows,) * 4,
        check_vma=False,
    )
```

time: 226 us -> 193 us (0.85)
  Pallas kernels: 71.2 us -> 38.9 us
    pallas_call x1, Pallas kernels: 68.7 us -> 36.4 us  [attention(): pl.pallas_call(attention_kernel, out_shape=(sds((32, 2, BLK, HD), BF16),...]
  transfers between devices with their start and end apart: 12 -> 12, of which waited for: 7 -> 9; matrix products, arithmetic and copies ran while one was open for 7% -> 8% of each run, Pallas kernels for 1% -> 1%
where the time goes in v2:
time: 193 us; the launch traced here: 191 us
  waiting for transfers between devices  61.3 us (32%)
  starting transfers between devices  51.4 us (27%)
  Pallas kernels  38.9 us (20%)
  local copies, waits for them, and re-layouts  19.5 us (10%)
  between operations  13.8 us (7%)
  other arithmetic  5.69 us (3%)
    all_to_all x4, waiting for transfers between devices, exchange(): return lax.all_to_all(x, GROUP, 0, 0, tiled=True)  37.8 us
    pallas_call x1, Pallas kernels, attention(): pl.pallas_call(attention_kernel, out_shape=(sds((32, 2, BLK, HD), BF16),...  36.4 us
    all_to_all x4, starting transfers between devices, exchange(): return lax.all_to_all(x, GROUP, 0, 0, tiled=True)  30.7 us
    slice x6, local copies, waits for them, and re-layouts, to_rows(): return (pair[0], pair[1])  10 us
    ppermute x1, waiting for transfers between devices, shards(): other = lax.ppermute(mine, 'y', PAIR_ONE)  9.04 us
    ppermute x1, waiting for transfers between devices, shards(): back_a = lax.ppermute(back_a, 'y', [(1, 0), (2, 1), (3, 2)])  8.5 us
    another operation x4, local copies, waits for them, and re-layouts, to_heads(): pair = jnp.stack([x, y], axis=0).reshape(2, BLK, 16, 2, HD)  6.37 us
    ppermute x1, starting transfers between devices, shards(): other = lax.ppermute(glob_grad, 'y', PAIR_ONE)  4.66 us
  transfers between devices with their start and end apart: 12, of which 9 were waited for; matrix products, arithmetic and copies ran while one was open for 8% of the time, Pallas kernels for 1%

profile of v2, /device:TPU:1, one launch (start us, length us, event | category | flops | bytes accessed | tf_op | source)
XLA Modules:
  0.0 190.6 jit_solution(14416175567062133392)
XLA Ops:
  0.6 1.7 copy.10
  2.4 0.4 copy.11
  2.8 1.5 pad_maximum_fusion
  4.3 9.6 %all-to-all-start = ((bf16[32,2,128,128]{3,2,1,0:T(8,128)(2,1)}), bf16[32,2,128,128]{3,2,1,0:T(8,128)(2,1)S(1)}, u32[]{:S(2)}, u32[]{:S(2)}) async-start(bf16[32,2,128,128]{3,2,1,0:T(8,128)(2,1)} %bitcast.9), calls=%async_computation | async-start | bytes 4194304 | tf_op jit(solution)/shard_map/all_to_all | solution.py:315
  13.9 0.7 fusion.5
  22.4 1.6 copy.12
  24.0 2.6 %copy.13 = bf16[1,128,16,2,128]{4,1,0,2,3:T(8,128)(2,1)} copy(bf16[1,128,16,2,128]{4,3,2,1,0:T(2,128)(2,1)} %bitcast.36) | data formatting | bytes 2097152 | tf_op jit(solution)/shard_map/stack | solution.py:303
  30.5 2.8 %pad_maximum_fusion.1 = bf16[2,128,16,2,128]{4,1,0,2,3:T(8,128)(2,1)} fusion(bf16[1,128,16,2,128]{4,1,0,2,3:T(8,128)(2,1)} %copy.13, bf16[1,128,16,2,128]{4,1,0,2,3:T(8,128)(2,1)S(1)} %copy.12), kind=kLoop, calls=%fused_computation.1 | loop fusion | flops 1048576 | bytes 4194304 | tf_op jit(solution)/shard_map/stack | solution.py:303
  33.3 8.9 %all-to-all-done.kv = bf16[32,2,128,128]{3,2,1,0:T(8,128)(2,1)S(1)} async-done(((bf16[32,2,128,128]{3,2,1,0:T(8,128)(2,1)}), bf16[32,2,128,128]{3,2,1,0:T(8,128)(2,1)S(1)}, u32[]{:S(2)}, u32[]{:S(2)}) %all-to-all-start) | async-done | bytes 2097184 | tf_op jit(solution)/shard_map/all_to_all | solution.py:315
  42.2 5.2 %all-to-all-start.1 = ((bf16[32,2,128,128]{3,2,1,0:T(8,128)(2,1)}), bf16[32,2,128,128]{3,2,1,0:T(8,128)(2,1)}, u32[]{:S(2)}, u32[]{:S(2)}) async-start(bf16[32,2,128,128]{3,2,1,0:T(8,128)(2,1)} %bitcast.13), calls=%async_computation.1 | async-start | bytes 4194304 | tf_op jit(solution)/shard_map/all_to_all | solution.py:315
  47.4 0.0 copy-start.3
  47.6 1.4 collective-permute-start.2
  49.0 9.0 %collective-permute-done.2 = bf16[6,2,128,128]{3,2,1,0:T(8,128)(2,1)S(1)} collective-permute-done((bf16[6,2,128,128]{3,2,1,0:T(8,128)(2,1)S(1)}, bf16[6,2,128,128]{3,2,1,0:T(8,128)(2,1)S(1)}, u32[]{:S(2)}, u32[]{:S(2)}) %collective-permute-start.2) | collective-permute-done | bytes 393248 | tf_op jit(solution)/shard_map/ppermute | solution.py:340
  58.0 0.1 broadcast_select_fusion
  58.1 2.8 %collective-permute-start.3 = (bf16[6,2,128,128]{3,2,1,0:T(8,128)(2,1)S(1)}, bf16[6,2,128,128]{3,2,1,0:T(8,128)(2,1)}, u32[]{:S(2)}, u32[]{:S(2)}) collective-permute-start(bf16[6,2,128,128]{3,2,1,0:T(8,128)(2,1)S(1)} %broadcast_select_fusion), channel_id=1, source_target_pairs={{32,64},{64,32},{96,0},{0,96},{33,65},{65,33},{97,1},{1,97},{34,66... | collective-permute-start | bytes 1179656 | tf_op jit(solution)/shard_map/ppermute | solution.py:342
  61.0 0.1 fusion.4
  61.1 1.3 collective-permute-start.1
  62.4 4.0 %collective-permute-start = (bf16[7,2,128,128]{3,2,1,0:T(8,128)(2,1)S(1)}, bf16[7,2,128,128]{3,2,1,0:T(8,128)(2,1)S(1)}, u32[]{:S(2)}, u32[]{:S(2)}) collective-permute-start(bf16[7,2,128,128]{3,2,1,0:T(8,128)(2,1)S(1)} %get-tuple-element.23), channel_id=1, source_target_pairs={{0,32},{32,64},{64,96},{1,33},{33,65},{65,97},{2,34},{34,66},{66,9... | collective-permute-start | bytes 1376264 | tf_op jit(solution)/shard_map/ppermute | solution.py:337
  66.4 0.6 fusion.6
  68.3 0.1 concatenate.8.info
  68.4 0.8 collective-permute-done.3
  69.1 1.1 broadcast_select_fusion.1.glob
  70.2 5.6 %all-to-all-done.1.qd = bf16[32,2,128,128]{3,2,1,0:T(8,128)(2,1)} async-done(((bf16[32,2,128,128]{3,2,1,0:T(8,128)(2,1)}), bf16[32,2,128,128]{3,2,1,0:T(8,128)(2,1)}, u32[]{:S(2)}, u32[]{:S(2)}) %all-to-all-start.1) | async-done | bytes 2097184 | tf_op jit(solution)/shard_map/all_to_all | solution.py:315
  75.8 0.0 collective-permute-done.1.halo_b
  75.9 0.0 collective-permute-done.halo_a
  75.9 0.8 copy-done.5
  76.6 0.8 copy-done.6
  77.4 36.4 %attention.1 = (bf16[32,2,128,128]{3,2,1,0:T(8,128)(2,1)}, bf16[32,2,128,128]{3,2,1,0:T(8,128)(2,1)}, bf16[7,2,128,128]{3,2,1,0:T(8,128)(2,1)S(1)}, bf16[7,2,128...) custom-call(s32[22]{0:T(128)S(1)} %concatenate.8.info, bf16[32,2,128,128]{3,2,1,0:T(8,128)(2,1)} %copy-done.1, ...), custom_call_target="tpu_custom_call" | custom-call | flops 11274289152 | bytes 16777216 | tf_op jit(solution)/shard_map/attention/pallas_call | solution.py:231
  113.8 7.8 %all-to-all-start.2 = ((bf16[32,2,128,128]{3,2,1,0:T(8,128)(2,1)}), bf16[32,2,128,128]{3,2,1,0:T(8,128)(2,1)}, u32[]{:S(2)}, u32[]{:S(2)}) async-start(bf16[32,2,128,128]{3,2,1,0:T(8,128)(2,1)} %get-tuple-element.9), calls=%async_computation.2 | async-start | bytes 4194304 | tf_op jit(solution)/shard_map/all_to_all | solution.py:315
  121.6 4.7 %collective-permute-start.6 = (bf16[6,2,128,128]{3,2,1,0:T(8,128)(2,1)S(1)}, bf16[6,2,128,128]{3,2,1,0:T(8,128)(2,1)S(1)}, u32[]{:S(2)}, u32[]{:S(2)}) collective-permute-start(bf16[6,2,128,128]{3,2,1,0:T(8,128)(2,1)S(1)} %get-tuple-element.13), channel_id=1, source_target_pairs={{0,32},{32,0},{64,96},{96,64},{1,33},{33,1},{65,97},{97,65},{2,34}... | collective-permute-start | bytes 1179656 | tf_op jit(solution)/shard_map/ppermute | solution.py:350
  126.3 1.3 collective-permute-start.4
  127.6 4.0 %collective-permute-start.5 = (bf16[7,2,128,128]{3,2,1,0:T(8,128)(2,1)S(1)}, bf16[7,2,128,128]{3,2,1,0:T(8,128)(2,1)S(1)}, u32[]{:S(2)}, u32[]{:S(2)}) collective-permute-start(bf16[7,2,128,128]{3,2,1,0:T(8,128)(2,1)S(1)} %get-tuple-element.12), channel_id=1, source_target_pairs={{0,32},{32,64},{64,96},{1,33},{33,65},{65,97},{2,34},{34,66},{66,9... | collective-permute-start | bytes 1376264 | tf_op jit(solution)/shard_map/ppermute | solution.py:349
  131.6 4.0 %collective-permute-done.6 = bf16[6,2,128,128]{3,2,1,0:T(8,128)(2,1)S(1)} collective-permute-done((bf16[6,2,128,128]{3,2,1,0:T(8,128)(2,1)S(1)}, bf16[6,2,128,128]{3,2,1,0:T(8,128)(2,1)S(1)}, u32[]{:S(2)}, u32[]{:S(2)}) %collective-permute-start.6) | collective-permute-done | bytes 393248 | tf_op jit(solution)/shard_map/ppermute | solution.py:350
  135.6 0.1 add_convert_fusion.glob_one
  135.7 1.2 collective-permute-start.7
  137.0 8.5 %collective-permute-done.4.back_a = bf16[7,2,128,128]{3,2,1,0:T(8,128)(2,1)S(1)} collective-permute-done((bf16[7,2,128,128]{3,2,1,0:T(8,128)(2,1)S(1)}, bf16[7,2,128,128]{3,2,1,0:T(8,128)(2,1)S(1)}, u32[]{:S(2)}, u32[]{:S(2)}) %collective-permute-start.4) | collective-permute-done | bytes 458784 | tf_op jit(solution)/shard_map/ppermute | solution.py:348
  145.5 0.0 collective-permute-done.5.back_b
  145.5 1.2 collective-permute-done.7.glob_two
  146.6 2.5 %finish.1 = bf16[32,2,128,128]{3,2,1,0:T(8,128)(2,1)} custom-call(s32[22]{0:T(128)S(1)} %concatenate.8.info, bf16[32,2,128,128]{3,2,1,0:T(8,128)(2,1)S(1)} %copy-done, bf16[7,2,128,128]{3,2,1,0:T(8,128)(2,1)S(1)} %collective-permute-done.4.back_a, bf16[7,2,128,128]{3,2,1,0:T(8,128)(2,1)S(1)} %collective-permute-done.5.back_b, ...), custom_call_target="tpu_custom_call" | custom-call | flops 2097152 | bytes 6291456 | tf_op jit(solution)/shard_map/finish/pallas_call | solution.py:291
  149.1 0.8 all-to-all-done.2
  150.0 8.1 %all-to-all-start.3 = ((bf16[32,2,128,128]{3,2,1,0:T(8,128)(2,1)}), bf16[32,2,128,128]{3,2,1,0:T(8,128)(2,1)S(1)}, u32[]{:S(2)}, u32[]{:S(2)}) async-start(bf16[32,2,128,128]{3,2,1,0:T(8,128)(2,1)} %finish.1), calls=%async_computation.3 | async-start | bytes 4194304 | tf_op jit(solution)/shard_map/all_to_all | solution.py:315
  158.1 1.7 fusion.3
  159.7 2.0 %copy.15 = bf16[1,128,16,2,128]{4,3,2,1,0:T(2,128)(2,1)} copy(bf16[1,128,16,2,128]{4,1,0,2,3:T(8,128)(2,1)S(1)} %get-tuple-element.20) | data formatting | bytes 2097152 | tf_op jit(solution)/shard_map/slice | solution.py:311
  161.8 2.0 %copy.14 = bf16[1,128,16,2,128]{4,3,2,1,0:T(2,128)(2,1)} copy(bf16[1,128,16,2,128]{4,1,0,2,3:T(8,128)(2,1)S(1)} %get-tuple-element.21) | data formatting | bytes 2097152 | tf_op jit(solution)/shard_map/slice | solution.py:311
  163.8 22.5 %all-to-all-done.3 = bf16[32,2,128,128]{3,2,1,0:T(8,128)(2,1)S(1)} async-done(((bf16[32,2,128,128]{3,2,1,0:T(8,128)(2,1)}), bf16[32,2,128,128]{3,2,1,0:T(8,128)(2,1)S(1)}, u32[]{:S(2)}, u32[]{:S(2)}) %all-to-all-start.3) | async-done | bytes 2097184 | tf_op jit(solution)/shard_map/all_to_all | solution.py:315
  186.4 0.1 fusion.2
  186.5 2.0 %copy.17 = bf16[1,128,16,2,128]{4,3,2,1,0:T(2,128)(2,1)} copy(bf16[1,128,16,2,128]{4,1,0,2,3:T(8,128)(2,1)S(1)} %get-tuple-element.18) | data formatting | bytes 2097152 | tf_op jit(solution)/shard_map/slice | solution.py:311
  188.5 2.0 %copy.16 = bf16[1,128,16,2,128]{4,3,2,1,0:T(2,128)(2,1)} copy(bf16[1,128,16,2,128]{4,1,0,2,3:T(8,128)(2,1)S(1)} %get-tuple-element.19) | data formatting | bytes 2097152 | tf_op jit(solution)/shard_map/slice | solution.py:311
  (20 shorter events, 0.2 us)
Async XLA Ops:
  0.6 1.7 copy-start.2
  4.3 9.6 %copy-start.4 = (s32[6]{0:T(128)S(1)}, s32[6]{0:T(128)}, u32[]{:S(2)}) copy-start(s32[6]{0:T(128)} %param.11) | copy-start | bytes 76
  4.3 37.9 %all-to-all-start = ((bf16[32,2,128,128]{3,2,1,0:T(8,128)(2,1)}), bf16[32,2,128,128]{3,2,1,0:T(8,128)(2,1)S(1)}, u32[]{:S(2)}, u32[]{:S(2)}) async-start(bf16[32,2,128,128]{3,2,1,0:T(8,128)(2,1)} %bitcast.9), calls=%async_computation | async-start | bytes 4194304 | tf_op jit(solution)/shard_map/all_to_all | solution.py:315
  42.2 18.8 %copy-start.1 = (bf16[32,2,128,128]{3,2,1,0:T(8,128)(2,1)}, bf16[32,2,128,128]{3,2,1,0:T(8,128)(2,1)S(1)}, u32[]{:S(2)}) copy-start(bf16[32,2,128,128]{3,2,1,0:T(8,128)(2,1)S(1)} %all-to-all-done.kv) | copy-start | bytes 6291460
  42.2 33.6 %all-to-all-start.1 = ((bf16[32,2,128,128]{3,2,1,0:T(8,128)(2,1)}), bf16[32,2,128,128]{3,2,1,0:T(8,128)(2,1)}, u32[]{:S(2)}, u32[]{:S(2)}) async-start(bf16[32,2,128,128]{3,2,1,0:T(8,128)(2,1)} %bitcast.13), calls=%async_computation.1 | async-start | bytes 4194304 | tf_op jit(solution)/shard_map/all_to_all | solution.py:315
  47.4 19.0 %copy-start.3 = (s32[2]{0:T(128)S(1)}, s32[2]{0:T(128)}, u32[]{:S(2)}) copy-start(s32[2]{0:T(128)} %param.10) | copy-start | bytes 28
  47.6 10.5 %collective-permute-start.2 = (bf16[6,2,128,128]{3,2,1,0:T(8,128)(2,1)S(1)}, bf16[6,2,128,128]{3,2,1,0:T(8,128)(2,1)S(1)}, u32[]{:S(2)}, u32[]{:S(2)}) collective-permute-start(bf16[6,2,128,128]{3,2,1,0:T(8,128)(2,1)S(1)} %dynamic-slice_dynamic-update-slice_fusion), channel_id=1, source_target_pairs={{0,32},{32,0},{64,96},{96,64},{1,33},{33,1},{65,97},{97,65},{2,34}... | collective-permute-start | bytes 1179656 | tf_op jit(solution)/shard_map/ppermute | solution.py:340
  58.1 11.0 %collective-permute-start.3 = (bf16[6,2,128,128]{3,2,1,0:T(8,128)(2,1)S(1)}, bf16[6,2,128,128]{3,2,1,0:T(8,128)(2,1)}, u32[]{:S(2)}, u32[]{:S(2)}) collective-permute-start(bf16[6,2,128,128]{3,2,1,0:T(8,128)(2,1)S(1)} %broadcast_select_fusion), channel_id=1, source_target_pairs={{32,64},{64,32},{96,0},{0,96},{33,65},{65,33},{97,1},{1,97},{34,66... | collective-permute-start | bytes 1179656 | tf_op jit(solution)/shard_map/ppermute | solution.py:342
  61.1 14.8 %collective-permute-start.1 = (bf16[7,2,128,128]{3,2,1,0:T(8,128)(2,1)S(1)}, bf16[7,2,128,128]{3,2,1,0:T(8,128)(2,1)S(1)}, u32[]{:S(2)}, u32[]{:S(2)}) collective-permute-start(bf16[7,2,128,128]{3,2,1,0:T(8,128)(2,1)S(1)} %get-tuple-element.22), channel_id=1, source_target_pairs={{96,64},{64,32},{32,0},{97,65},{65,33},{33,1},{98,66},{66,34},{34,... | collective-permute-start | bytes 1376264 | tf_op jit(solution)/shard_map/ppermute | solution.py:338
  62.4 13.5 %collective-permute-start = (bf16[7,2,128,128]{3,2,1,0:T(8,128)(2,1)S(1)}, bf16[7,2,128,128]{3,2,1,0:T(8,128)(2,1)S(1)}, u32[]{:S(2)}, u32[]{:S(2)}) collective-permute-start(bf16[7,2,128,128]{3,2,1,0:T(8,128)(2,1)S(1)} %get-tuple-element.23), channel_id=1, source_target_pairs={{0,32},{32,64},{64,96},{1,33},{33,65},{65,97},{2,34},{34,66},{66,9... | collective-permute-start | bytes 1376264 | tf_op jit(solution)/shard_map/ppermute | solution.py:337
  75.9 0.8 copy-start.5
  76.6 0.8 copy-start.6
  113.8 32.9 %copy-start = (bf16[32,2,128,128]{3,2,1,0:T(8,128)(2,1)S(1)}, bf16[32,2,128,128]{3,2,1,0:T(8,128)(2,1)}, u32[]{:S(2)}) copy-start(bf16[32,2,128,128]{3,2,1,0:T(8,128)(2,1)} %get-tuple-element.10.own) | copy-start | bytes 6291460
  113.8 36.2 %all-to-all-start.2 = ((bf16[32,2,128,128]{3,2,1,0:T(8,128)(2,1)}), bf16[32,2,128,128]{3,2,1,0:T(8,128)(2,1)}, u32[]{:S(2)}, u32[]{:S(2)}) async-start(bf16[32,2,128,128]{3,2,1,0:T(8,128)(2,1)} %get-tuple-element.9), calls=%async_computation.2 | async-start | bytes 4194304 | tf_op jit(solution)/shard_map/all_to_all | solution.py:315
  121.6 14.0 %collective-permute-start.6 = (bf16[6,2,128,128]{3,2,1,0:T(8,128)(2,1)S(1)}, bf16[6,2,128,128]{3,2,1,0:T(8,128)(2,1)S(1)}, u32[]{:S(2)}, u32[]{:S(2)}) collective-permute-start(bf16[6,2,128,128]{3,2,1,0:T(8,128)(2,1)S(1)} %get-tuple-element.13), channel_id=1, source_target_pairs={{0,32},{32,0},{64,96},{96,64},{1,33},{33,1},{65,97},{97,65},{2,34}... | collective-permute-start | bytes 1179656 | tf_op jit(solution)/shard_map/ppermute | solution.py:350
  126.3 19.2 %collective-permute-start.4 = (bf16[7,2,128,128]{3,2,1,0:T(8,128)(2,1)S(1)}, bf16[7,2,128,128]{3,2,1,0:T(8,128)(2,1)S(1)}, u32[]{:S(2)}, u32[]{:S(2)}) collective-permute-start(bf16[7,2,128,128]{3,2,1,0:T(8,128)(2,1)S(1)} %get-tuple-element.11), channel_id=1, source_target_pairs={{32,0},{64,32},{96,64},{33,1},{65,33},{97,65},{34,2},{66,34},{98,6... | collective-permute-start | bytes 1376264 | tf_op jit(solution)/shard_map/ppermute | solution.py:348
  127.6 17.9 %collective-permute-start.5 = (bf16[7,2,128,128]{3,2,1,0:T(8,128)(2,1)S(1)}, bf16[7,2,128,128]{3,2,1,0:T(8,128)(2,1)S(1)}, u32[]{:S(2)}, u32[]{:S(2)}) collective-permute-start(bf16[7,2,128,128]{3,2,1,0:T(8,128)(2,1)S(1)} %get-tuple-element.12), channel_id=1, source_target_pairs={{0,32},{32,64},{64,96},{1,33},{33,65},{65,97},{2,34},{34,66},{66,9... | collective-permute-start | bytes 1376264 | tf_op jit(solution)/shard_map/ppermute | solution.py:349
  135.7 10.9 %collective-permute-start.7 = (bf16[6,2,128,128]{3,2,1,0:T(8,128)(2,1)S(1)}, bf16[6,2,128,128]{3,2,1,0:T(8,128)(2,1)S(1)}, u32[]{:S(2)}, u32[]{:S(2)}) collective-permute-start(bf16[6,2,128,128]{3,2,1,0:T(8,128)(2,1)S(1)} %add_convert_fusion.glob_one), channel_id=1, source_target_pairs={{32,64},{64,32},{96,0},{0,96},{33,65},{65,33},{97,1},{1,97},{34,66... | collective-permute-start | bytes 1179656 | tf_op jit(solution)/shard_map/ppermute | solution.py:352
  150.0 36.4 %all-to-all-start.3 = ((bf16[32,2,128,128]{3,2,1,0:T(8,128)(2,1)}), bf16[32,2,128,128]{3,2,1,0:T(8,128)(2,1)S(1)}, u32[]{:S(2)}, u32[]{:S(2)}) async-start(bf16[32,2,128,128]{3,2,1,0:T(8,128)(2,1)} %finish.1), calls=%async_computation.3 | async-start | bytes 4194304 | tf_op jit(solution)/shard_map/all_to_all | solution.py:315
